TPU v7x, 128 devices: a whole 4x4x4 slice. The times are simulated.
128 devices in a mesh: row: 8 (over y_hi, z), col: 16 (over y_lo, x, core).
Axes of the slice: x: 4, y: 4 (y_hi: 2, y_lo: 2; y = y_hi * 2 + y_lo), z: 4, core: 2. Of those that a mesh axis runs over, the one named last changes fastest.
Arguments:
- iterate: float32 [6144, 4096], P('row', 'col'), may hold values from -6 to 6
- factor: float32 [4096, 4096], P(None, 'col'), may hold values from -0.0625 to 0.0625
- inverses: float32 [8, 512, 512], replicated, as said below
Outputs:
- gram_matrix: float32 [4096, 4096], P('row', 'col')
- panel_factor: float32 [4096, 512], P(('row', 'col'))
- solved: float32 [6144, 4096], P('row', 'col')
Inputs may be any that keep to these rules, and one draw needn't show every extreme that they name: Each block of inverses is upper triangular with positive diagonal entries.
All inputs are finite; a program needn't handle non-finite values.
Results may differ from a plain program's by a relative error of at most 0.00013.
Values sent between devices are 32-bit elements; how exact they have to be, the bound alone decides.
A program may use at most 128 MiB of HBM per device.

v0:
```python
import jax
import jax.numpy as jnp
from jax import lax
from jax.sharding import PartitionSpec as P


def from_root(block, axis, source):
    block = jnp.where(lax.axis_index(axis) == source, block, jnp.zeros_like(block))
    return lax.psum(block, axis)


def on_device(iterate, factor, inverses):
    highest = lax.Precision.HIGHEST
    row_dev, local_width = iterate.shape
    n_rows = lax.axis_size("row")
    n_cols = lax.axis_size("col")
    full_order = local_width * n_cols
    panel_width = inverses.shape[1]
    panels = inverses.shape[0]
    owners = panel_width // local_width
    row_index = lax.axis_index("row")
    col_index = lax.axis_index("col")
    scale_factor = 3.0 / (row_dev * n_rows)
    block_rows = full_order // n_rows
    gathered = lax.all_gather(iterate, "col", axis=1, tiled=True)
    summed = lax.psum_scatter(
        lax.dot_general(
            gathered,
            iterate,
            (((0,), (0,)), ((), ())),
            precision=highest,
            preferred_element_type=jnp.float32,
        ),
        "row",
        scatter_dimension=0,
        tiled=True,
    )
    row_ids = row_index * block_rows + jnp.arange(block_rows)[:, None]
    col_ids = col_index * local_width + jnp.arange(local_width)[None, :]
    gram_block = jnp.where(row_ids == col_ids, 1.0, 0.0).astype(jnp.float32) + scale_factor * summed
    offset = jnp.minimum(col_index * local_width, panel_width - local_width)
    empty = jnp.zeros((block_rows, panel_width), jnp.float32)
    placed = lax.dynamic_update_slice_in_dim(empty, gram_block, offset, 1)
    placed = jnp.where(col_index < owners, placed, 0.0)
    panel_rows = lax.psum(placed, "col")
    leading_rows = from_root(panel_rows, "row", 0)
    leading = jnp.linalg.cholesky(leading_rows)
    share_rows = block_rows // n_cols
    my_rows = lax.dynamic_slice_in_dim(panel_rows, col_index * share_rows, share_rows, 0)
    panel_factor = jax.scipy.linalg.solve_triangular(leading, my_rows.T, lower=True).T
    pending = iterate
    solved = jnp.zeros_like(iterate)
    for panel_idx in range(panels):
        pieces = []
        for owner_idx in range(owners):
            pieces.append(from_root(pending, "col", panel_idx * owners + owner_idx))
        current = jnp.concatenate(pieces, axis=1)
        offset = jnp.clip(
            col_index * local_width - panel_idx * panel_width, 0, panel_width - local_width
        )
        is_owner = (col_index >= panel_idx * owners) & (col_index < (panel_idx + 1) * owners)
        later_cols = col_ids >= (panel_idx + 1) * panel_width
        result = jnp.dot(
            current, inverses[panel_idx], precision=highest, preferred_element_type=jnp.float32
        )
        my_cols = lax.dynamic_slice_in_dim(result, offset, local_width, 1)
        solved = jnp.where(is_owner, my_cols, solved)
        if panel_idx + 1 < panels:
            coupling = factor[panel_idx * panel_width : (panel_idx + 1) * panel_width]
            update = jnp.dot(
                result, coupling, precision=highest, preferred_element_type=jnp.float32
            )
            pending = pending - jnp.where(later_cols, update, 0.0)
    return (gram_block, panel_factor, solved)


def solution(mesh):
    placed = (P("row", "col"), P(None, "col"), P())
    return jax.shard_map(
        on_device,
        mesh=mesh,
        in_specs=placed,
        out_specs=(P("row", "col"), P(("row", "col"), None), P("row", "col")),
        check_vma=False,
    )
```

profile of v0, /device:TPU:14, one launch (start us, length us, event | category | flops | bytes accessed | tf_op | source)
XLA Modules:
  0.0 1449.8 jit_solution(17881885991674394439)
XLA Ops:
  9.7 121.4 %all-reduce.35.cloned.1.call-done = (f32[768,256]{1,0:T(8,128)}, f32[768,256]{1,0:T(8,128)}) async-done(((f32[768,256]{1,0:T(8,128)}, f32[768,256]{1,0:T(8,128)}), (f32[768,256]{1,0:T(8,128)}, f32[768,256]{1,0:T(8,128)})) %all-reduce.35.cloned.1.call-update) | async-done | bytes 1572880 | tf_op jit(solution)/shard_map/psum | solution.py:9
  131.1 4.4 fusion
  139.2 122.5 %all-reduce.33.cloned.1.call-done = (f32[768,256]{1,0:T(8,128)}, f32[768,256]{1,0:T(8,128)}) async-done(((f32[768,256]{1,0:T(8,128)}, f32[768,256]{1,0:T(8,128)}), (f32[768,256]{1,0:T(8,128)}, f32[768,256]{1,0:T(8,128)})) %all-reduce.33.cloned.1.call-update) | async-done | bytes 1572880 | tf_op jit(solution)/shard_map/psum | solution.py:9
  261.7 4.3 fusion.4
  270.3 122.3 %all-reduce.31.cloned.1.call-done = (f32[768,256]{1,0:T(8,128)}, f32[768,256]{1,0:T(8,128)}) async-done(((f32[768,256]{1,0:T(8,128)}, f32[768,256]{1,0:T(8,128)}), (f32[768,256]{1,0:T(8,128)}, f32[768,256]{1,0:T(8,128)})) %all-reduce.31.cloned.1.call-update) | async-done | bytes 1572880 | tf_op jit(solution)/shard_map/psum | solution.py:9
  392.6 4.3 fusion.8
  401.1 122.5 %all-reduce.29.cloned.1.call-done = (f32[768,256]{1,0:T(8,128)}, f32[768,256]{1,0:T(8,128)}) async-done(((f32[768,256]{1,0:T(8,128)}, f32[768,256]{1,0:T(8,128)}), (f32[768,256]{1,0:T(8,128)}, f32[768,256]{1,0:T(8,128)})) %all-reduce.29.cloned.1.call-update) | async-done | bytes 1572880 | tf_op jit(solution)/shard_map/psum | solution.py:9
  523.5 4.3 fusion.12
  527.9 4.3 broadcast_select_fusion.8
  532.3 122.4 %all-reduce.27.cloned.1.call-done = (f32[768,256]{1,0:T(8,128)}, f32[768,256]{1,0:T(8,128)}) async-done(((f32[768,256]{1,0:T(8,128)}, f32[768,256]{1,0:T(8,128)}), (f32[768,256]{1,0:T(8,128)}, f32[768,256]{1,0:T(8,128)})) %all-reduce.27.cloned.1.call-update) | async-done | bytes 1572880 | tf_op jit(solution)/shard_map/psum | solution.py:9
  654.7 4.4 fusion.16
  659.2 4.0 broadcast_select_fusion.6
  664.5 121.2 %all-reduce.25.cloned.1.call-done = (f32[768,256]{1,0:T(8,128)}, f32[768,256]{1,0:T(8,128)}) async-done(((f32[768,256]{1,0:T(8,128)}, f32[768,256]{1,0:T(8,128)}), (f32[768,256]{1,0:T(8,128)}, f32[768,256]{1,0:T(8,128)})) %all-reduce.25.cloned.1.call-update) | async-done | bytes 1572880 | tf_op jit(solution)/shard_map/psum | solution.py:9
  785.8 4.3 fusion.20
  794.2 69.1 %all-gather.2.cloned.1.call-done = f32[768,4096]{1,0:T(8,128)} async-done(((f32[768,256]{1,0:T(8,128)}), f32[768,4096]{1,0:T(8,128)}) %all-gather.2.cloned.1.call-update) | async-done | bytes 12582928 | tf_op jit(solution)/shard_map/all_gather | solution.py:25
  863.3 15.5 %fusion.108 = f32[4096,256]{0,1:T(8,128)} fusion(f32[768,4096]{1,0:T(8,128)} %all-gather.2.cloned.1.call-done, f32[768,256]{1,0:T(8,128)S(1)} %copy-done.1), kind=kOutput, calls=%fused_computation.174 | convolution fusion | flops 9663676416 | bytes 17563648 | tf_op jit(solution)/shard_map/dot_general | solution.py:27
  878.9 106.8 %all-reduce.23.cloned.1.call-done = (f32[768,256]{1,0:T(8,128)}, f32[768,256]{1,0:T(8,128)}) async-done(((f32[768,256]{1,0:T(8,128)}, f32[768,256]{1,0:T(8,128)}), (f32[768,256]{1,0:T(8,128)}, f32[768,256]{1,0:T(8,128)})) %all-reduce.23.cloned.1.call-update) | async-done | bytes 1572880 | tf_op jit(solution)/shard_map/psum | solution.py:9
  985.6 4.3 fusion.24
  994.8 83.8 %reduce-scatter.2.cloned.1.call-done = f32[512,256]{0,1:T(8,128)} async-done(((f32[4096,256]{0,1:T(8,128)}), f32[512,256]{0,1:T(8,128)}) %reduce-scatter.2.cloned.1.call-update) | async-done | bytes 524304 | tf_op jit(solution)/shard_map/reduce_scatter | solution.py:26
  1082.5 120.6 %all-reduce.21.cloned.1.call-done = (f32[512,512]{0,1:T(8,128)}, f32[768,256]{1,0:T(8,128)}, f32[768,256]{1,0:T(8,128)}) async-done(((f32[512,512]{0,1:T(8,128)}, f32[768,256]{1,0:T(8,128)}, f32[768,256]{1,0:T(8,128)}), (f32[512,512]{0,1:T(8,128)}, f32[768,256]{1,0:T(8,128)}, f32[768,256]{1,0:T(8,128)})) %all-reduce.21.cloned.1.call-update) | async-done | bytes 2621456 | tf_op jit(solution)/shard_map/psum | solution.py:45
  1208.8 4.5 fusion.28
  1213.3 4.3 select_select_fusion.1
  1217.6 79.8 %all-reduce.19.cloned.1.call-done = f32[512,512]{0,1:T(8,128)} async-done(((f32[512,512]{0,1:T(8,128)}), f32[512,512]{0,1:T(8,128)}) %all-reduce.19.cloned.1.call-update) | async-done | bytes 1048592 | tf_op jit(solution)/shard_map/psum | solution.py:9
  1300.3 11.7 cholesky.103
  1312.2 9.8 custom-call.31
  1324.6 11.9 cholesky.215
  1336.7 9.8 custom-call.32
  1348.5 11.7 cholesky.236
  1360.4 10.0 custom-call.33
  1372.0 11.7 cholesky.253
  1388.8 11.0 while.1
  1399.8 40.1 %custom-call.34 = f32[4,128,128]{1,2,0:T(8,128)S(1)} custom-call(f32[4,128,128]{2,1,0:T(8,128)} %get-tuple-element.10), custom_call_target="InvertDiagBlocksLowerTriangular" | custom-call | tf_op jit(solution)/shard_map/jit(_solve_triangular)/triangular_solve | solution.py:50
  (133 shorter events, 59.8 us)
Async XLA Ops:
  7.2 123.9 %all-reduce.35.cloned.1.call-start = ((), (), s32[]{:S(2)}) async-start(), calls=%async_computation.11 | async-start | bytes 3145728 | tf_op jit(solution)/shard_map/psum | solution.py:9
  9.6 252.0 %all-reduce.33.cloned.1.call-start = ((), (), s32[]{:S(2)}) async-start(), calls=%async_computation.10 | async-start | bytes 3145728 | tf_op jit(solution)/shard_map/psum | solution.py:9
  131.1 4.4 copy-start
  139.1 253.5 %all-reduce.31.cloned.1.call-start = ((), (), s32[]{:S(2)}) async-start(), calls=%async_computation.9 | async-start | bytes 3145728 | tf_op jit(solution)/shard_map/psum | solution.py:9
  266.0 4.0 copy-start.2
  270.1 253.5 %all-reduce.29.cloned.1.call-start = ((), (), s32[]{:S(2)}) async-start(), calls=%async_computation.8 | async-start | bytes 3145728 | tf_op jit(solution)/shard_map/psum | solution.py:9
  396.9 4.0 copy-start.4
  401.0 253.7 %all-reduce.27.cloned.1.call-start = ((), (), s32[]{:S(2)}) async-start(), calls=%async_computation.7 | async-start | bytes 3145728 | tf_op jit(solution)/shard_map/psum | solution.py:9
  527.9 4.3 copy-start.6
  532.2 253.6 %all-reduce.25.cloned.1.call-start = ((), (), s32[]{:S(2)}) async-start(), calls=%async_computation.6 | async-start | bytes 3145728 | tf_op jit(solution)/shard_map/psum | solution.py:9
  654.7 4.4 copy-start.13
  659.1 4.1 copy-start.8
  663.2 200.1 %all-gather.2.cloned.1.call-start = ((), (), s32[]{:S(2)}) async-start(), calls=%async_computation.1 | async-start | bytes 13369344 | tf_op jit(solution)/shard_map/all_gather | solution.py:25
  664.0 321.7 %all-reduce.23.cloned.1.call-start = ((), (), s32[]{:S(2)}) async-start(), calls=%async_computation.5 | async-start | bytes 3145728 | tf_op jit(solution)/shard_map/psum | solution.py:9
  790.1 4.0 copy-start.9
  794.1 69.2 %copy-start.1 = (f32[768,256]{1,0:T(8,128)S(1)}, f32[768,256]{1,0:T(8,128)}, u32[]{:S(2)}) copy-start(f32[768,256]{1,0:T(8,128)} %param.3) | copy-start | bytes 2359300
  794.1 284.5 %reduce-scatter.2.cloned.1.call-start = ((), (), s32[]{:S(2)}) async-start(), calls=%async_computation.2 | async-start | bytes 4718592 | tf_op jit(solution)/shard_map/reduce_scatter | solution.py:26
  878.8 324.3 %all-reduce.21.cloned.1.call-start = ((), (), s32[]{:S(2)}) async-start(), calls=%async_computation.4 | async-start | bytes 5242880 | tf_op jit(solution)/shard_map/psum | solution.py:45
  990.0 1.2 copy-start.10
  1081.2 1.0 copy-start.12
  1082.2 215.2 %all-reduce.19.cloned.1.call-start = ((), (), s32[]{:S(2)}) async-start(), calls=%async_computation.3 | async-start | bytes 2097152 | tf_op jit(solution)/shard_map/psum | solution.py:9
  1205.5 7.8 copy-start.7
  1208.8 4.5 copy-start.3
  1208.8 4.5 copy-start.5
  1297.4 1.7 copy-start.11
  1299.3 1.0 copy-start.14
Sparse Core Ops, SparseCore 0:
  11.1 119.9 all-reduce.34
  139.3 122.3 all-reduce.32
  270.2 122.3 all-reduce.30
  401.1 122.3 all-reduce.28
  532.3 122.3 all-reduce.26
  663.3 122.3 all-reduce.24
  787.4 75.8 all-gather.1
  866.4 119.1 all-reduce.22
  989.9 88.5 reduce-scatter.1
  1082.4 120.6 all-reduce.20
  1205.6 91.7 all-reduce.18
where the time goes:
time: 1460 us; the launch traced here: 1450 us
  waiting for transfers between devices  1190 us (82%)
  other arithmetic  131 us (9%)
  matrix products  86.1 us (6%)
  local copies, waits for them, and re-layouts  20.3 us (1%)
  between operations  17.7 us (1%)
    psum x8, waiting for transfers between devices, from_root(): return lax.psum(block, axis)  919 us
    psum x1, waiting for transfers between devices, on_device(): panel_rows = lax.psum(placed, 'col')  121 us
    reduce_scatter x1, waiting for transfers between devices, on_device(): lax.psum_scatter(lax.dot_general(gathered, iterate, (((0,), (0,)), ((), (...  83.8 us
    another operation x14, other arithmetic, on_device(): leading = jnp.linalg.cholesky(leading_rows)  78.9 us
    all_gather x1, waiting for transfers between devices, on_device(): gathered = lax.all_gather(iterate, 'col', axis=1, tiled=True)  69.1 us
    another operation x3, other arithmetic, on_device(): jax.scipy.linalg.solve_triangular(leading, my_rows.T, lower=True)  40.3 us
    dot_general x8, matrix products, on_device(): jnp.dot(current, inverses[panel_idx], precision=highest, preferred_elemen...  35 us
  transfers between devices with their start and end apart: 11, of which 11 were waited for; matrix products, arithmetic and copies ran while one was open for 3% of the time, Pallas kernels for 0%

commit v1 on v0

--- a/solution.py
+++ b/solution.py
@@ -1,7 +1,179 @@
+import functools
+
 import jax
 import jax.numpy as jnp
 from jax import lax
+from jax.experimental import pallas as pl
+from jax.experimental.pallas import tpu as pltpu
 from jax.sharding import PartitionSpec as P
+
+ROUTES = (
+    ((0, 1), (0, 3), (0, 4), (1, 2), (1, 5), (4, 7), (7, 6)),
+    ((1, 2), (1, 5), (2, 3), (2, 6), (5, 4), (6, 7)),
+    ((2, 3), (2, 6), (3, 7), (6, 5), (7, 4)),
+    ((3, 7), (7, 4), (7, 6), (6, 5)),
+    ((4, 5), (4, 7), (5, 6)),
+    ((5, 6), (6, 7)),
+    ((6, 7),),
+    (),
+)
+CHIPS = 8
+CHUNKS = 6
+SLOTS = 5
+MESH = pl.DeviceIdType.MESH
+
+
+def split(value):
+    high = value.astype(jnp.bfloat16)
+    return high, (value - high.astype(jnp.float32)).astype(jnp.bfloat16)
+
+
+def dot3(left, right_high, right_low):
+    high, low = split(left)
+    dot = functools.partial(jnp.dot, preferred_element_type=jnp.float32)
+    return dot(high, right_high) + (dot(high, right_low) + dot(low, right_high))
+
+
+def solve_kernel(base_ref, high_ref, low_ref, out_ref, panels, part, part_in, send, recv, part_send, part_recv):
+    row = lax.axis_index("row")
+    col = lax.axis_index("col")
+    chip = col // 2
+    core = col % 2
+    width = out_ref.shape[1]
+    rows = out_ref.shape[0] // CHUNKS
+    sibling = (row, 2 * chip + 1 - core)
+
+    barrier = pltpu.get_barrier_semaphore()
+    for step in range(1, CHIPS):
+        pl.semaphore_signal(
+            barrier, inc=1, device_id=(row, 2 * ((chip + step) % CHIPS) + core), device_id_type=MESH
+        )
+    pl.semaphore_signal(barrier, inc=1, device_id=sibling, device_id_type=MESH)
+    pl.semaphore_wait(barrier, CHIPS)
+
+    def run(me):
+        onward = [[b for a, b in ROUTES[j] if a == me] for j in range(CHIPS)]
+        slots = {}
+        for j in range(CHIPS):
+            for target in onward[j]:
+                slots[j, target] = len(slots)
+        early = 4 if me >= 4 else 0
+        lag = me - early
+
+        def window(t):
+            return pl.ds(pl.multiple_of(t * rows, rows), rows)
+
+        def transfer(j, target, t):
+            source = out_ref.at[window(t)] if j == me else panels.at[j, window(t)]
+            return pltpu.make_async_remote_copy(
+                src_ref=source,
+                dst_ref=panels.at[j, window(t)],
+                send_sem=send.at[slots.get((j, target), 0), t],
+                recv_sem=recv.at[j, t],
+                device_id=(row, 2 * target + core),
+                device_id_type=MESH,
+            )
+
+        def exchange(t):
+            return pltpu.make_async_remote_copy(
+                src_ref=part.at[t, 1 - core],
+                dst_ref=part_in.at[t],
+                send_sem=part_send.at[t],
+                recv_sem=part_recv.at[t],
+                device_id=sibling,
+                device_id_type=MESH,
+            )
+
+        def arrive(j, t):
+            transfer(j, (me + 1) % CHIPS, t).wait_recv()
+            for target in onward[j]:
+                transfer(j, target, t).start()
+
+        def finish(t):
+            total = base_ref[window(t)]
+            for j in range(me):
+                if j >= early:
+                    arrive(j, t)
+                span = pl.ds(j * width, width)
+                total = total - dot3(panels[j, window(t)], high_ref[span], low_ref[span])
+            part[t, 0] = total[:, :width]
+            part[t, 1] = total[:, width:]
+            exchange(t).start()
+            exchange(t).wait_recv()
+            out_ref[window(t)] = part[t, core] + part_in[t]
+            for target in onward[me]:
+                transfer(me, target, t).start()
+
+        def step(tick, carry):
+            if early:
+
+                @pl.when(tick < CHUNKS)
+                def _():
+                    for j in range(early):
+                        arrive(j, tick)
+
+                @pl.when(tick >= lag)
+                def _():
+                    finish(tick - lag)
+
+            else:
+                finish(tick)
+            return carry
+
+        lax.fori_loop(0, CHUNKS + lag, step, 0) if early else lax.fori_loop(0, CHUNKS, step, 0)
+
+        def drain(t, carry):
+            exchange(t).wait_send()
+            for j, target in slots:
+                transfer(j, target, t).wait_send()
+            return carry
+
+        lax.fori_loop(0, CHUNKS, drain, 0)
+
+    for me in range(CHIPS):
+        pl.when(chip == me)(functools.partial(run, me))
+
+
+def solve(iterate, factor, inverses):
+    n_rows, width = iterate.shape
+    order, _ = factor.shape
+    rows = n_rows // CHUNKS
+    high = lax.Precision.HIGH
+    chip = lax.axis_index("col") // 2
+    core = lax.axis_index("col") % 2
+    inverse = lax.dynamic_index_in_dim(inverses, chip, 0, keepdims=False)
+    blocks = factor.reshape(CHIPS, 2, width, width)
+    mine = lax.dynamic_index_in_dim(blocks, core, 1, keepdims=False).reshape(order // 2, width)
+    theirs = lax.dynamic_index_in_dim(blocks, 1 - core, 1, keepdims=False).reshape(order // 2, width)
+    pairs = [(c, c ^ 1) for c in range(2 * CHIPS)]
+    theirs = lax.ppermute(theirs, "col", pairs)
+    both = jnp.where(core == 0, jnp.concatenate([mine, theirs], 1), jnp.concatenate([theirs, mine], 1))
+    coupling = jnp.dot(both, inverse, precision=high, preferred_element_type=jnp.float32)
+    rounded = lax.reduce_precision(coupling, 8, 7)
+    w_high = rounded.astype(jnp.bfloat16)
+    w_low = (coupling - rounded).astype(jnp.bfloat16)
+    half = lax.dynamic_slice_in_dim(inverse, core * width, width, 0)
+    base = jnp.dot(iterate, half, precision=high, preferred_element_type=jnp.float32)
+    vmem = pl.BlockSpec(memory_space=pltpu.VMEM)
+    return pl.pallas_call(
+        solve_kernel,
+        out_shape=jax.ShapeDtypeStruct((n_rows, width), jnp.float32),
+        in_specs=[vmem] * 3,
+        out_specs=vmem,
+        scratch_shapes=[
+            pltpu.VMEM((CHIPS - 1, n_rows, width), jnp.float32),
+            pltpu.VMEM((CHUNKS, 2, rows, width), jnp.float32),
+            pltpu.VMEM((CHUNKS, rows, width), jnp.float32),
+            pltpu.SemaphoreType.DMA((SLOTS, CHUNKS)),
+            pltpu.SemaphoreType.DMA((CHIPS, CHUNKS)),
+            pltpu.SemaphoreType.DMA((CHUNKS,)),
+            pltpu.SemaphoreType.DMA((CHUNKS,)),
+        ],
+        compiler_params=pltpu.CompilerParams(
+            collective_id=0, has_side_effects=True, vmem_limit_bytes=40 << 20
+        ),
+        cost_estimate=pl.CostEstimate(flops=3 * 10**9, bytes_accessed=10**7, transcendentals=0),
+    )(base, w_high, w_low)
 
 
 def from_root(block, axis, source):
@@ -48,29 +220,7 @@
     share_rows = block_rows // n_cols
     my_rows = lax.dynamic_slice_in_dim(panel_rows, col_index * share_rows, share_rows, 0)
     panel_factor = jax.scipy.linalg.solve_triangular(leading, my_rows.T, lower=True).T
-    pending = iterate
-    solved = jnp.zeros_like(iterate)
-    for panel_idx in range(panels):
-        pieces = []
-        for owner_idx in range(owners):
-            pieces.append(from_root(pending, "col", panel_idx * owners + owner_idx))
-        current = jnp.concatenate(pieces, axis=1)
-        offset = jnp.clip(
-            col_index * local_width - panel_idx * panel_width, 0, panel_width - local_width
-        )
-        is_owner = (col_index >= panel_idx * owners) & (col_index < (panel_idx + 1) * owners)
-        later_cols = col_ids >= (panel_idx + 1) * panel_width
-        result = jnp.dot(
-            current, inverses[panel_idx], precision=highest, preferred_element_type=jnp.float32
-        )
-        my_cols = lax.dynamic_slice_in_dim(result, offset, local_width, 1)
-        solved = jnp.where(is_owner, my_cols, solved)
-        if panel_idx + 1 < panels:
-            coupling = factor[panel_idx * panel_width : (panel_idx + 1) * panel_width]
-            update = jnp.dot(
-                result, coupling, precision=highest, preferred_element_type=jnp.float32
-            )
-            pending = pending - jnp.where(later_cols, update, 0.0)
+    solved = solve(iterate, factor, inverses)
     return (gram_block, panel_factor, solved)
 
 

time: 1460 us -> 671 us (0.46)
  waiting for transfers between devices: 1190 us -> 271 us
  Pallas kernels: 0 us -> 193 us
  matrix products: 86.1 us -> 28.8 us
    psum x8 -> x1, waiting for transfers between devices: 919 us -> 0.02 us  [from_root(): return lax.psum(block, axis)]
    pallas_call x0 -> x1, Pallas kernels: none -> 193 us  [solve(): pl.pallas_call(solve_kernel, out_shape=jax.ShapeDtypeStruct((n_rows, widt...]
    dot_general x15 -> x2, matrix products: 62.5 us -> 7.92 us  [the longest x1 6.04 us: solve(): jnp.dot(both, inverse, precision=high, preferred_element_type=jnp.float32)]
  transfers between devices with their start and end apart: 11 -> 5, of which waited for: 11 -> 3; matrix products, arithmetic and copies ran while one was open for 3% -> 3% of each run, Pallas kernels for 0% -> 29%
where the time goes in v1:
time: 671 us; the launch traced here: 664 us
  waiting for transfers between devices  271 us (40%)
  Pallas kernels  193 us (29%)
  other arithmetic  127 us (19%)
  matrix products  28.8 us (4%)
  local copies, waits for them, and re-layouts  25.6 us (4%)
  between operations  17.1 us (3%)
    pallas_call x1, Pallas kernels, solve(): pl.pallas_call(solve_kernel, out_shape=jax.ShapeDtypeStruct((n_rows, widt...  193 us
    psum x1, waiting for transfers between devices, on_device(): panel_rows = lax.psum(placed, 'col')  115 us
    another operation x14, other arithmetic, on_device(): leading = jnp.linalg.cholesky(leading_rows)  80.9 us
    reduce_scatter x1, waiting for transfers between devices, on_device(): lax.psum_scatter(lax.dot_general(gathered, iterate, (((0,), (0,)), ((), (...  80.7 us
    all_gather x1, waiting for transfers between devices, on_device(): gathered = lax.all_gather(iterate, 'col', axis=1, tiled=True)  75.1 us
    another operation x3, other arithmetic, on_device(): jax.scipy.linalg.solve_triangular(leading, my_rows.T, lower=True)  40.3 us
    dot_general x1, matrix products, on_device(): lax.dot_general(gathered, iterate, (((0,), (0,)), ((), ())), precision=hi...  15.6 us
  transfers between devices with their start and end apart: 5, of which 3 were waited for; matrix products, arithmetic and copies ran while one was open for 3% of the time, Pallas kernels for 29%

profile of v1, /device:TPU:14, one launch (start us, length us, event | category | flops | bytes accessed | tf_op | source)
XLA Modules:
  0.0 664.2 jit_solution(10622333483249436161)
XLA Ops:
  7.9 75.1 %all-gather.2.cloned.1.call-done = f32[768,4096]{1,0:T(8,128)} async-done(((f32[768,256]{1,0:T(8,128)}), f32[768,4096]{1,0:T(8,128)}) %all-gather.2.cloned.1.call-update) | async-done | bytes 12582928 | tf_op jit(solution)/shard_map/all_gather | solution.py:197
  83.0 15.6 %fusion.46 = f32[4096,256]{0,1:T(8,128)} fusion(f32[768,4096]{1,0:T(8,128)} %all-gather.2.cloned.1.call-done, f32[768,256]{1,0:T(8,128)} %param.3), kind=kOutput, calls=%fused_computation.94 | convolution fusion | flops 9663676416 | bytes 17563648 | tf_op jit(solution)/shard_map/dot_general | solution.py:199
  98.7 4.6 constant_dynamic-slice_fusion.2
  103.5 80.7 %reduce-scatter.2.cloned.1.call-done = f32[512,256]{0,1:T(8,128)} async-done(((f32[4096,256]{0,1:T(8,128)}), f32[512,256]{0,1:T(8,128)}) %reduce-scatter.2.cloned.1.call-update) | async-done | bytes 524304 | tf_op jit(solution)/shard_map/reduce_scatter | solution.py:198
  184.2 1.2 broadcast_select_fusion.1
  186.1 1.0 copy-done.1
  187.6 114.9 %all-reduce.4.cloned.1.call-done = f32[512,512]{0,1:T(8,128)} async-done(((f32[512,512]{0,1:T(8,128)}), f32[512,512]{0,1:T(8,128)}) %all-reduce.4.cloned.1.call-update) | async-done | bytes 1048592 | tf_op jit(solution)/shard_map/psum | solution.py:217
  302.5 2.4 broadcast_select_fusion
  305.0 1.9 convolution_bitcast_fusion.base_ref
  306.9 6.0 fusion
  313.0 193.4 %shard_map.58 = f32[768,256]{1,0:T(8,128)S(1)} custom-call(f32[768,512]{1,0:T(8,128)S(1)} %convolution_bitcast_fusion.base_ref, bf16[2048,512]{1,0:T(8,128)(2,1)S(1)} %get-tuple-element.31.high_ref, bf16[2048,512]{1,0:T(8,128)(2,1)S(1)} %get-tuple-element.30.low_ref), custom_call_target="tpu_custom_call" | custom-call | flops 3000000000 | bytes 10000000 | tf_op jit(solution)/shard_map/pallas_call | solution.py:158
  506.4 1.0 copy.17
  507.4 1.1 dynamic-slice_bitcast_fusion
  508.5 1.6 copy.7
  510.0 1.4 fusion.9
  511.5 11.7 %cholesky.103 = f32[128,128]{1,0:T(8,128)S(1)} custom-call(f32[128,128]{1,0:T(8,128)S(1)} %cholesky.263), custom_call_target="Cholesky" | custom-call | tf_op jit(solution)/shard_map/jit(cholesky)/cholesky | solution.py:219
  524.0 9.8 %custom-call.31 = f32[1,128,128]{1,2,0:T(8,128)S(1)} custom-call(f32[1,128,128]{2,1,0:T(8,128)S(1)} %get-tuple-element.39), custom_call_target="InvertDiagBlocksLowerTriangular" | custom-call | tf_op jit(solution)/shard_map/jit(cholesky)/cholesky | solution.py:219
  534.6 11.7 %cholesky.215 = f32[128,128]{1,0:T(8,128)S(1)} custom-call(f32[128,128]{1,0:T(8,128)S(1)} %cholesky.267), custom_call_target="Cholesky" | custom-call | tf_op jit(solution)/shard_map/jit(cholesky)/cholesky | solution.py:219
  547.7 1.0 cholesky.222
  548.6 11.5 %custom-call.32 = f32[1,128,128]{1,2,0:T(8,128)} custom-call(f32[1,128,128]{2,1,0:T(8,128)} %get-tuple-element.37), custom_call_target="InvertDiagBlocksLowerTriangular" | custom-call | tf_op jit(solution)/shard_map/jit(cholesky)/cholesky | solution.py:219
  560.1 0.8 constant_dynamic-update-slice_fusion.2
  561.0 1.2 convolution_dynamic-update-slice_fusion
  562.7 11.7 %cholesky.236 = f32[128,128]{1,0:T(8,128)S(1)} custom-call(f32[128,128]{1,0:T(8,128)S(1)} %cholesky.272), custom_call_target="Cholesky" | custom-call | tf_op jit(solution)/shard_map/jit(cholesky)/cholesky | solution.py:219
  574.6 9.8 %custom-call.33 = f32[1,128,128]{1,2,0:T(8,128)S(1)} custom-call(f32[1,128,128]{2,1,0:T(8,128)S(1)} %get-tuple-element.35), custom_call_target="InvertDiagBlocksLowerTriangular" | custom-call | tf_op jit(solution)/shard_map/jit(cholesky)/cholesky | solution.py:219
  585.2 11.9 %cholesky.253 = f32[128,128]{1,0:T(8,128)S(1)} custom-call(f32[128,128]{1,0:T(8,128)S(1)} %convolution_subtract_fusion.5), custom_call_target="Cholesky" | custom-call | tf_op jit(solution)/shard_map/jit(cholesky)/cholesky | solution.py:219
  602.0 11.4 %while.1 = (s32[]{:T(128)}, f32[512,512]{0,1:T(8,128)S(1)}, s32[4,2]{0,1:T(2,128)S(1)}, f32[4,128,128]{2,1,0:T(8,128)}, s32[]{:T(128)}) while((s32[]{:T(128)}, f32[512,512]{0,1:T(8,128)S(1)}, s32[4,2]{0,1:T(2,128)S(1)}, f32[4,128,128]{2,1,0:T(8,128)}, s32[]{:T(128)}) %tuple.32), condition=%wide.while_cond, body=%wide.while_body.sunk | while | flops 2 | bytes 393329 | solution.py:222
  602.7 1.4 dynamic-slice.11
  605.5 1.4 dynamic-slice.11
  608.4 1.4 dynamic-slice.11
  611.2 1.4 dynamic-slice.11
  613.4 40.1 %custom-call.34 = f32[4,128,128]{1,2,0:T(8,128)S(1)} custom-call(f32[4,128,128]{2,1,0:T(8,128)} %get-tuple-element.10), custom_call_target="InvertDiagBlocksLowerTriangular" | custom-call | tf_op jit(solution)/shard_map/jit(_solve_triangular)/triangular_solve | solution.py:222
  656.4 0.9 copy.43
  (71 shorter events, 17.4 us)
Async XLA Ops:
  7.2 75.8 %all-gather.2.cloned.1.call-start = ((), (), s32[]{:S(2)}) async-start(), calls=%async_computation.1 | async-start | bytes 13369344 | tf_op jit(solution)/shard_map/all_gather | solution.py:197
  7.9 176.3 %reduce-scatter.2.cloned.1.call-start = ((), (), s32[]{:S(2)}) async-start(), calls=%async_computation.2 | async-start | bytes 4718592 | tf_op jit(solution)/shard_map/reduce_scatter | solution.py:198
  98.6 203.9 %all-reduce.4.cloned.1.call-start = ((), (), s32[]{:S(2)}) async-start(), calls=%async_computation.3 | async-start | bytes 2097152 | tf_op jit(solution)/shard_map/psum | solution.py:217
  103.2 201.8 %copy-start = (f32[768,256]{1,0:T(8,128)S(1)}, f32[768,256]{1,0:T(8,128)}, u32[]{:S(2)}) copy-start(f32[768,256]{1,0:T(8,128)} %param.3) | copy-start | bytes 2359300
  103.2 203.7 %collective-permute-start = (f32[2048,256]{1,0:T(8,128)}, f32[2048,256]{1,0:T(8,128)}, u32[]{:S(2)}, u32[]{:S(2)}) collective-permute-start(f32[2048,256]{1,0:T(8,128)} %bitcast.17), channel_id=1, source_target_pairs={{0,1},{1,0},{2,3},{3,2},{4,5},{5,4},{6,7},{7,6},{8,9},{9,8},{10,11... | collective-permute-start | bytes 6291464 | tf_op jit(solution)/shard_map/ppermute | solution.py:149
  186.1 1.0 copy-start.1
  187.1 119.9 %copy-start.2 = (f32[8,1,256,256]{3,2,1,0:T(8,128)S(1)}, f32[8,1,256,256]{3,2,1,0:T(8,128)}, u32[]{:S(2)}) copy-start(f32[8,1,256,256]{3,2,1,0:T(8,128)} %get-tuple-element.32) | copy-start | bytes 6291460
  187.1 321.4 %all-reduce.6.cloned.1.call-start = ((), (), s32[]{:S(2)}) async-start(), calls=%async_computation.4 | async-start | bytes 2097152 | tf_op jit(solution)/shard_map/psum | solution.py:181
Sparse Core Ops, SparseCore 0:
  9.7 73.3 all-gather.1
  98.7 85.4 reduce-scatter.1
  187.2 115.3 all-reduce.3
  305.1 93.7 all-reduce.5

commit v2 on v1

--- a/solution.py
+++ b/solution.py
@@ -20,6 +20,7 @@
 CHIPS = 8
 CHUNKS = 6
 SLOTS = 5
+LAG = 4
 MESH = pl.DeviceIdType.MESH
 
 
@@ -58,7 +59,10 @@
             for target in onward[j]:
                 slots[j, target] = len(slots)
         early = 4 if me >= 4 else 0
-        lag = me - early
+        stages = [(0, [j for j in range(early) if j + 4 in (me, me - 1)])]
+        stages.append((2, [j for j in range(early) if j not in stages[0][1] and onward[j]]))
+        relayed = stages[0][1] + stages[1][1]
+        lag = LAG if early else 0
 
         def window(t):
             return pl.ds(pl.multiple_of(t * rows, rows), rows)
@@ -92,7 +96,7 @@
         def finish(t):
             total = base_ref[window(t)]
             for j in range(me):
-                if j >= early:
+                if j not in relayed:
                     arrive(j, t)
                 span = pl.ds(j * width, width)
                 total = total - dot3(panels[j, window(t)], high_ref[span], low_ref[span])
@@ -105,22 +109,21 @@
                 transfer(me, target, t).start()
 
         def step(tick, carry):
-            if early:
-
-                @pl.when(tick < CHUNKS)
-                def _():
-                    for j in range(early):
-                        arrive(j, tick)
-
-                @pl.when(tick >= lag)
-                def _():
-                    finish(tick - lag)
-
+            for delay, sources in stages:
+                if sources:
+
+                    @pl.when((tick >= delay) & (tick < CHUNKS + delay))
+                    def _():
+                        for j in sources:
+                            arrive(j, tick - delay)
+
+            if lag:
+                pl.when(tick >= lag)(lambda: finish(tick - lag))
             else:
                 finish(tick)
             return carry
 
-        lax.fori_loop(0, CHUNKS + lag, step, 0) if early else lax.fori_loop(0, CHUNKS, step, 0)
+        lax.fori_loop(0, CHUNKS + lag, step, 0)
 
         def drain(t, carry):
             exchange(t).wait_send()

time: 671 us -> 575 us (0.86)
  Pallas kernels: 193 us -> 97.4 us
    pallas_call x1, Pallas kernels: 193 us -> 97.4 us  [solve(): pl.pallas_call(solve_kernel, out_shape=jax.ShapeDtypeStruct((n_rows, widt...]
  transfers between devices with their start and end apart: 5 -> 5, of which waited for: 3 -> 3; matrix products, arithmetic and copies ran while one was open for 3% -> 3% of each run, Pallas kernels for 29% -> 17%
where the time goes in v2:
time: 575 us; the launch traced here: 568 us
  waiting for transfers between devices  271 us (47%)
  other arithmetic  127 us (22%)
  Pallas kernels  97.4 us (17%)
  matrix products  28.8 us (5%)
  local copies, waits for them, and re-layouts  25.6 us (4%)
  between operations  17.1 us (3%)
    psum x1, waiting for transfers between devices, on_device(): panel_rows = lax.psum(placed, 'col')  115 us
    pallas_call x1, Pallas kernels, solve(): pl.pallas_call(solve_kernel, out_shape=jax.ShapeDtypeStruct((n_rows, widt...  97.4 us
    another operation x14, other arithmetic, on_device(): leading = jnp.linalg.cholesky(leading_rows)  80.9 us
    reduce_scatter x1, waiting for transfers between devices, on_device(): lax.psum_scatter(lax.dot_general(gathered, iterate, (((0,), (0,)), ((), (...  80.7 us
    all_gather x1, waiting for transfers between devices, on_device(): gathered = lax.all_gather(iterate, 'col', axis=1, tiled=True)  75.1 us
    another operation x3, other arithmetic, on_device(): jax.scipy.linalg.solve_triangular(leading, my_rows.T, lower=True)  40.3 us
    dot_general x1, matrix products, on_device(): lax.dot_general(gathered, iterate, (((0,), (0,)), ((), ())), precision=hi...  15.6 us
  transfers between devices with their start and end apart: 5, of which 3 were waited for; matrix products, arithmetic and copies ran while one was open for 3% of the time, Pallas kernels for 17%

profile of v2, /device:TPU:14, one launch (start us, length us, event | category | flops | bytes accessed | tf_op | source)
XLA Modules:
  0.0 568.2 jit_solution(16348299046242504422)
XLA Ops:
  7.9 75.1 %all-gather.2.cloned.1.call-done = f32[768,4096]{1,0:T(8,128)} async-done(((f32[768,256]{1,0:T(8,128)}), f32[768,4096]{1,0:T(8,128)}) %all-gather.2.cloned.1.call-update) | async-done | bytes 12582928 | tf_op jit(solution)/shard_map/all_gather | solution.py:200
  83.0 15.6 %fusion.46 = f32[4096,256]{0,1:T(8,128)} fusion(f32[768,4096]{1,0:T(8,128)} %all-gather.2.cloned.1.call-done, f32[768,256]{1,0:T(8,128)} %param.3), kind=kOutput, calls=%fused_computation.94 | convolution fusion | flops 9663676416 | bytes 17563648 | tf_op jit(solution)/shard_map/dot_general | solution.py:202
  98.7 4.6 constant_dynamic-slice_fusion.2
  103.5 80.7 %reduce-scatter.2.cloned.1.call-done = f32[512,256]{0,1:T(8,128)} async-done(((f32[4096,256]{0,1:T(8,128)}), f32[512,256]{0,1:T(8,128)}) %reduce-scatter.2.cloned.1.call-update) | async-done | bytes 524304 | tf_op jit(solution)/shard_map/reduce_scatter | solution.py:201
  184.2 1.2 broadcast_select_fusion.1
  186.1 1.0 copy-done.1
  187.6 114.9 %all-reduce.4.cloned.1.call-done = f32[512,512]{0,1:T(8,128)} async-done(((f32[512,512]{0,1:T(8,128)}), f32[512,512]{0,1:T(8,128)}) %all-reduce.4.cloned.1.call-update) | async-done | bytes 1048592 | tf_op jit(solution)/shard_map/psum | solution.py:220
  302.5 2.4 broadcast_select_fusion
  305.0 1.9 convolution_bitcast_fusion.base_ref
  306.9 6.0 %fusion = (bf16[2048,512]{1,0:T(8,128)(2,1)S(1)}, bf16[2048,512]{1,0:T(8,128)(2,1)S(1)}) fusion(f32[8,512,512]{2,1,0:T(8,128)} %param.5, s32[]{:T(128)S(6)} %select_n.79, f32[2048,256]{1,0:T(8,128)} %collective-permute-done, f32[2048,256]{1,0:T(8,128)S(1)} %bitcast.67, pred[]{:T(512)S(6)} %eq.25), kind=kOutput, calls=%fused_computation.4 | convolution fusion | flops 3228565504 | bytes 9437189 | tf_op jit(solution)/shard_map/dot_general | solution.py:154
  313.0 97.4 %shard_map.58 = f32[768,256]{1,0:T(8,128)S(1)} custom-call(f32[768,512]{1,0:T(8,128)S(1)} %convolution_bitcast_fusion.base_ref, bf16[2048,512]{1,0:T(8,128)(2,1)S(1)} %get-tuple-element.31.high_ref, bf16[2048,512]{1,0:T(8,128)(2,1)S(1)} %get-tuple-element.30.low_ref), custom_call_target="tpu_custom_call" | custom-call | flops 3000000000 | bytes 10000000 | tf_op jit(solution)/shard_map/pallas_call | solution.py:161
  410.3 1.0 copy.17
  411.3 1.1 dynamic-slice_bitcast_fusion
  412.4 1.6 copy.7
  414.0 1.4 fusion.9
  415.5 11.7 %cholesky.103 = f32[128,128]{1,0:T(8,128)S(1)} custom-call(f32[128,128]{1,0:T(8,128)S(1)} %cholesky.263), custom_call_target="Cholesky" | custom-call | tf_op jit(solution)/shard_map/jit(cholesky)/cholesky | solution.py:222
  428.0 9.8 %custom-call.31 = f32[1,128,128]{1,2,0:T(8,128)S(1)} custom-call(f32[1,128,128]{2,1,0:T(8,128)S(1)} %get-tuple-element.39), custom_call_target="InvertDiagBlocksLowerTriangular" | custom-call | tf_op jit(solution)/shard_map/jit(cholesky)/cholesky | solution.py:222
  438.6 11.7 %cholesky.215 = f32[128,128]{1,0:T(8,128)S(1)} custom-call(f32[128,128]{1,0:T(8,128)S(1)} %cholesky.267), custom_call_target="Cholesky" | custom-call | tf_op jit(solution)/shard_map/jit(cholesky)/cholesky | solution.py:222
  451.6 1.0 cholesky.222
  452.6 11.5 %custom-call.32 = f32[1,128,128]{1,2,0:T(8,128)} custom-call(f32[1,128,128]{2,1,0:T(8,128)} %get-tuple-element.37), custom_call_target="InvertDiagBlocksLowerTriangular" | custom-call | tf_op jit(solution)/shard_map/jit(cholesky)/cholesky | solution.py:222
  464.1 0.8 constant_dynamic-update-slice_fusion.2
  464.9 1.2 convolution_dynamic-update-slice_fusion
  466.7 11.7 %cholesky.236 = f32[128,128]{1,0:T(8,128)S(1)} custom-call(f32[128,128]{1,0:T(8,128)S(1)} %cholesky.272), custom_call_target="Cholesky" | custom-call | tf_op jit(solution)/shard_map/jit(cholesky)/cholesky | solution.py:222
  478.6 9.8 %custom-call.33 = f32[1,128,128]{1,2,0:T(8,128)S(1)} custom-call(f32[1,128,128]{2,1,0:T(8,128)S(1)} %get-tuple-element.35), custom_call_target="InvertDiagBlocksLowerTriangular" | custom-call | tf_op jit(solution)/shard_map/jit(cholesky)/cholesky | solution.py:222
  489.2 11.9 %cholesky.253 = f32[128,128]{1,0:T(8,128)S(1)} custom-call(f32[128,128]{1,0:T(8,128)S(1)} %convolution_subtract_fusion.5), custom_call_target="Cholesky" | custom-call | tf_op jit(solution)/shard_map/jit(cholesky)/cholesky | solution.py:222
  506.0 11.4 %while.1 = (s32[]{:T(128)}, f32[512,512]{0,1:T(8,128)S(1)}, s32[4,2]{0,1:T(2,128)S(1)}, f32[4,128,128]{2,1,0:T(8,128)}, s32[]{:T(128)}) while((s32[]{:T(128)}, f32[512,512]{0,1:T(8,128)S(1)}, s32[4,2]{0,1:T(2,128)S(1)}, f32[4,128,128]{2,1,0:T(8,128)}, s32[]{:T(128)}) %tuple.32), condition=%wide.while_cond, body=%wide.while_body.sunk | while | flops 2 | bytes 393329 | solution.py:225
  506.6 1.4 dynamic-slice.11
  509.5 1.4 dynamic-slice.11
  512.3 1.4 dynamic-slice.11
  515.2 1.4 dynamic-slice.11
  517.3 40.1 %custom-call.34 = f32[4,128,128]{1,2,0:T(8,128)S(1)} custom-call(f32[4,128,128]{2,1,0:T(8,128)} %get-tuple-element.10), custom_call_target="InvertDiagBlocksLowerTriangular" | custom-call | tf_op jit(solution)/shard_map/jit(_solve_triangular)/triangular_solve | solution.py:225
  560.3 0.9 copy.43
  (71 shorter events, 17.5 us)
Async XLA Ops:
  7.2 75.8 %all-gather.2.cloned.1.call-start = ((), (), s32[]{:S(2)}) async-start(), calls=%async_computation.1 | async-start | bytes 13369344 | tf_op jit(solution)/shard_map/all_gather | solution.py:200
  7.9 176.3 %reduce-scatter.2.cloned.1.call-start = ((), (), s32[]{:S(2)}) async-start(), calls=%async_computation.2 | async-start | bytes 4718592 | tf_op jit(solution)/shard_map/reduce_scatter | solution.py:201
  98.6 203.9 %all-reduce.4.cloned.1.call-start = ((), (), s32[]{:S(2)}) async-start(), calls=%async_computation.3 | async-start | bytes 2097152 | tf_op jit(solution)/shard_map/psum | solution.py:220
  103.2 201.8 %copy-start = (f32[768,256]{1,0:T(8,128)S(1)}, f32[768,256]{1,0:T(8,128)}, u32[]{:S(2)}) copy-start(f32[768,256]{1,0:T(8,128)} %param.3) | copy-start | bytes 2359300
  103.2 203.7 %collective-permute-start = (f32[2048,256]{1,0:T(8,128)}, f32[2048,256]{1,0:T(8,128)}, u32[]{:S(2)}, u32[]{:S(2)}) collective-permute-start(f32[2048,256]{1,0:T(8,128)} %bitcast.17), channel_id=1, source_target_pairs={{0,1},{1,0},{2,3},{3,2},{4,5},{5,4},{6,7},{7,6},{8,9},{9,8},{10,11... | collective-permute-start | bytes 6291464 | tf_op jit(solution)/shard_map/ppermute | solution.py:152
  186.1 1.0 copy-start.1
  187.1 119.9 %copy-start.2 = (f32[8,1,256,256]{3,2,1,0:T(8,128)S(1)}, f32[8,1,256,256]{3,2,1,0:T(8,128)}, u32[]{:S(2)}) copy-start(f32[8,1,256,256]{3,2,1,0:T(8,128)} %get-tuple-element.32) | copy-start | bytes 6291460
  187.1 225.4 %all-reduce.6.cloned.1.call-start = ((), (), s32[]{:S(2)}) async-start(), calls=%async_computation.4 | async-start | bytes 2097152 | tf_op jit(solution)/shard_map/psum | solution.py:184
Sparse Core Ops, SparseCore 0:
  9.7 73.3 all-gather.1
  98.7 85.4 reduce-scatter.1
  187.2 115.3 all-reduce.3
  305.1 93.7 all-reduce.5

commit v3 on v2

--- a/solution.py
+++ b/solution.py
@@ -35,7 +35,298 @@
     return dot(high, right_high) + (dot(high, right_low) + dot(low, right_high))
 
 
-def solve_kernel(base_ref, high_ref, low_ref, out_ref, panels, part, part_in, send, recv, part_send, part_recv):
+def gram_kernel(mine_ref, gram_ref, lead_ref, theirs, got, high, low, prod, land, slices, send, recv, push, landed, cut, cut_in, share, shared):
+    row = lax.axis_index("row")
+    col = lax.axis_index("col")
+    n_rows = lax.axis_size("row")
+    chip = col // 2
+    core = col % 2
+    x, y = chip % 4, chip // 4
+    n, width = mine_ref.shape
+    half = n // 2
+    piece = width // n_rows
+    scale = 3.0 / (n * n_rows)
+
+    def at(dx, dy):
+        return 4 * ((y + dy) % 2) + (x + dx) % 4
+
+    left, right, partner, far = at(3, 0), at(1, 0), at(0, 1), at(2, 0)
+    barrier = pltpu.get_barrier_semaphore()
+    for other in (2 * left + core, 2 * right + core, 2 * partner + core, 2 * chip + 1 - core):
+        pl.semaphore_signal(barrier, inc=1, device_id=(row, other), device_id_type=MESH)
+    for step in range(1, n_rows):
+        for other in range(2):
+            pl.semaphore_signal(
+                barrier, inc=1, device_id=((row + step) % n_rows, 2 * chip + other), device_id_type=MESH
+            )
+    pl.semaphore_wait(barrier, 4 + 2 * (n_rows - 1))
+
+    def copy(source, target, out, arrival, device):
+        return pltpu.make_async_remote_copy(
+            src_ref=source, dst_ref=target, send_sem=out, recv_sem=arrival, device_id=device, device_id_type=MESH
+        )
+
+    top, low_half = pl.ds(0, half), pl.ds(half, half)
+    at_right, at_left = (row, 2 * right + core), (row, 2 * left + core)
+    at_partner, at_sibling = (row, 2 * partner + core), (row, 2 * chip + 1 - core)
+    sends = [
+        copy(mine_ref, theirs, send.at[8], recv.at[8], at_sibling),
+        copy(mine_ref, got.at[chip], send.at[0], recv.at[0], at_right),
+        copy(mine_ref, got.at[chip], send.at[1], recv.at[1], at_left),
+        copy(mine_ref, got.at[chip], send.at[2], recv.at[2], at_partner),
+        copy(got.at[left, top], got.at[left, top], send.at[3], recv.at[3], at_right),
+        copy(got.at[right, low_half], got.at[right, low_half], send.at[4], recv.at[4], at_left),
+        copy(got.at[partner], got.at[partner], send.at[5], recv.at[5], at_right),
+        copy(got.at[partner], got.at[partner], send.at[6], recv.at[6], at_left),
+        copy(got.at[far], got.at[far], send.at[7], recv.at[7], at_partner),
+    ]
+    for one in sends[:4]:
+        one.start()
+    got[chip] = mine_ref[...]
+    own_high, own_low = split(mine_ref[...])
+    high[core] = own_high
+    low[core] = own_low
+    sends[0].wait_recv()
+    their_high, their_low = split(theirs[...])
+    high[1 - core] = their_high
+    low[1 - core] = their_low
+
+    def order(idx):
+        dx = jnp.where((idx == 1) | (idx == 5), 3, jnp.where((idx == 2) | (idx == 6), 1, jnp.where((idx == 4) | (idx == 7), 2, 0)))
+        dy = jnp.where((idx == 3) | (idx > 4), 1, 0)
+        return at(dx, dy)
+
+    def away(block, to):
+        return copy(
+            prod.at[block, to], land.at[row, core], push.at[block, to], landed.at[row, core], (block, 2 * chip + to)
+        )
+
+    def slice_to(other):
+        return copy(
+            prod.at[0, :, pl.ds(pl.multiple_of(other * piece, piece), piece)],
+            slices.at[row],
+            cut.at[other],
+            cut_in.at[row],
+            (other, core),
+        )
+
+    def lead_rows(at_row, at_core):
+        return lead_ref.at[pl.ds(pl.multiple_of(at_core * width + at_row * piece, piece), piece)]
+
+    def share_to(step, to):
+        return copy(
+            lead_rows(row, core), lead_rows(row, core), share.at[step, to], shared.at[row, core],
+            ((row + step) % n_rows, to),
+        )
+
+    def body(idx, carry):
+        @pl.when(idx == 1)
+        def _():
+            for one in sends[1:4]:
+                one.wait_recv()
+            for one in sends[4:8]:
+                one.start()
+
+        @pl.when(idx == 4)
+        def _():
+            sends[4].wait_recv()
+            sends[5].wait_recv()
+            sends[8].start()
+
+        @pl.when(idx > 4)
+        def _():
+            copy(mine_ref, got.at[chip], send.at[0], recv.at[idx], at_right).wait_recv()
+
+        block = order(idx)
+        left_high, left_low = split(got[block])
+        dot = functools.partial(
+            lax.dot_general, dimension_numbers=(((0,), (0,)), ((), ())), preferred_element_type=jnp.float32
+        )
+        for to in range(2):
+            prod[block, to] = dot(left_high, high[to]) + (dot(left_high, low[to]) + dot(left_low, high[to]))
+
+        @pl.when(block != row)
+        def _():
+            away(block, core).start()
+
+        @pl.when(block == row)
+        def _():
+            land[row, core] = prod[block, core]
+
+        away(block, 1 - core).start()
+
+        @pl.when((idx == 0) & (chip == 0))
+        def _():
+            for step in range(1, n_rows):
+                slice_to((row + step) % n_rows).start()
+            slices[row] = prod[0, :, pl.ds(pl.multiple_of(row * piece, piece), piece)]
+
+        @pl.when((idx == 3) & (chip == 0))
+        def _():
+            for step in range(1, n_rows):
+                source = (row + step) % n_rows
+                copy(
+                    slices.at[row], slices.at[source], cut.at[source], cut_in.at[source], (source, core)
+                ).wait_recv()
+            total = slices[0]
+            for other in range(1, n_rows):
+                total = total + slices[other]
+            whole = scale * jnp.concatenate([total[0], total[1]], axis=1)
+            first = core * width + row * piece
+            shape = (piece, 2 * width)
+            there = lax.broadcasted_iota(jnp.int32, shape, 0) + first == lax.broadcasted_iota(jnp.int32, shape, 1)
+            lead_rows(row, core)[...] = whole + jnp.where(there, 1.0, 0.0)
+            for step in range(n_rows):
+                for to in range(2):
+                    if step:
+                        share_to(step, to).start()
+            share_to(0, 1 - core).start()
+
+        return carry
+
+    lax.fori_loop(0, CHIPS, body, 0)
+
+    @pl.when(chip == 0)
+    def _():
+        for step in range(n_rows):
+            for other in range(2):
+                source = (row + step) % n_rows
+
+                @pl.when((step > 0) | (core != other))
+                def _():
+                    rows = lead_rows(source, other)
+                    copy(rows, rows, share.at[0, 0], shared.at[source, other], (source, 0)).wait_recv()
+
+        for step in range(1, n_rows):
+            slice_to((row + step) % n_rows).wait_send()
+            for to in range(2):
+                share_to(step, to).wait_send()
+        share_to(0, 1 - core).wait_send()
+
+    for other in range(2):
+        for step in range(n_rows):
+            source = (row + step) % n_rows
+
+            @pl.when((step > 0) | (core != other))
+            def _():
+                copy(
+                    prod.at[0, 0], land.at[source, other], push.at[0, 0], landed.at[source, other], at_sibling
+                ).wait_recv()
+
+        total = land[0, other]
+        for source in range(1, n_rows):
+            total = total + land[source, other]
+        shape = (width, width)
+        shift = (row * 2 + other - (2 * chip + core)) * width
+        there = lax.broadcasted_iota(jnp.int32, shape, 0) + shift == lax.broadcasted_iota(jnp.int32, shape, 1)
+        gram_ref[pl.ds(other * width, width)] = jnp.where(there, 1.0, 0.0) + scale * total
+
+    for one in sends:
+        one.wait_send()
+
+    def drain(block, carry):
+        pl.when(block != row)(lambda: away(block, core).wait_send())
+        away(block, 1 - core).wait_send()
+        return carry
+
+    lax.fori_loop(0, CHIPS, drain, 0)
+
+
+def gram(iterate):
+    n, width = iterate.shape
+    n_rows = lax.axis_size("row")
+    vmem = pl.BlockSpec(memory_space=pltpu.VMEM)
+    dma = pltpu.SemaphoreType.DMA
+    return pl.pallas_call(
+        gram_kernel,
+        out_shape=(
+            jax.ShapeDtypeStruct((2 * width, width), jnp.float32),
+            jax.ShapeDtypeStruct((2 * width, 2 * width), jnp.float32),
+        ),
+        in_specs=[vmem],
+        out_specs=(vmem, vmem),
+        scratch_shapes=[
+            pltpu.VMEM((n, width), jnp.float32),
+            pltpu.VMEM((CHIPS, n, width), jnp.float32),
+            pltpu.VMEM((2, n, width), jnp.bfloat16),
+            pltpu.VMEM((2, n, width), jnp.bfloat16),
+            pltpu.VMEM((CHIPS, 2, width, width), jnp.float32),
+            pltpu.VMEM((n_rows, 2, width, width), jnp.float32),
+            pltpu.VMEM((n_rows, 2, width // n_rows, width), jnp.float32),
+            dma((9,)),
+            dma((9,)),
+            dma((CHIPS, 2)),
+            dma((n_rows, 2)),
+            dma((n_rows,)),
+            dma((n_rows,)),
+            dma((n_rows, 2)),
+            dma((n_rows, 2)),
+        ],
+        compiler_params=pltpu.CompilerParams(
+            collective_id=1, has_side_effects=True, vmem_limit_bytes=48 << 20
+        ),
+        cost_estimate=pl.CostEstimate(flops=5 * 10**9, bytes_accessed=10**7, transcendentals=0),
+    )(iterate)
+
+
+def factor_block(grid):
+    base = grid.shape[0]
+    for p in range(base // 8):
+        rows = slice(8 * p, 8 * p + 8)
+        panel = grid[rows]
+        sub = lax.broadcasted_iota(jnp.int32, panel.shape, 0)
+        columns = [jnp.broadcast_to(panel[:, 8 * p + c : 8 * p + c + 1], panel.shape) for c in range(8)]
+        scales = jnp.zeros_like(panel)
+        for j in range(8):
+            pivot = jnp.broadcast_to(columns[j][j : j + 1], panel.shape)
+            guess = lax.rsqrt(pivot)
+            guess = guess * (1.5 - 0.5 * pivot * guess * guess)
+            below = jnp.where(sub > j, columns[j] * (guess * guess), 0.0)
+            scales = jnp.where(sub == j, guess, scales)
+            for c in range(j + 1, 8):
+                columns[c] = columns[c] - below * columns[c][j : j + 1]
+            panel = panel - below * panel[j : j + 1]
+        panel = panel * scales
+        grid[rows] = panel
+        if 8 * p + 8 < base:
+            rest = slice(8 * p + 8, base)
+            turned = panel[:, :base].T[8 * p + 8 :]
+            value = grid[rest]
+            for j in range(8):
+                value = value - turned[:, j : j + 1] * panel[j : j + 1]
+            grid[rest] = value
+
+
+def panel_solve(work, grid, size):
+    base = grid.shape[0]
+    highest = lax.Precision.HIGHEST
+    dims = (((1,), (1,)), ((), ()))
+
+    def block(s, carry):
+        span = pl.ds(pl.multiple_of(s * base, base), base)
+        shape = (base, base)
+        eye = lax.broadcasted_iota(jnp.int32, shape, 0) == lax.broadcasted_iota(jnp.int32, shape, 1)
+        grid[:, :base] = work[span, span]
+        grid[:, base:] = jnp.where(eye, 1.0, 0.0)
+        factor_block(grid)
+        done = lax.dot_general(
+            work[:, span], grid[:, base:], dims, precision=highest, preferred_element_type=jnp.float32
+        )
+        below = lax.broadcasted_iota(jnp.int32, done.shape, 0) >= (s + 1) * base
+        done = jnp.where(below, done, 0.0)
+        work[...] = work[...] - lax.dot_general(
+            done, done[:size], dims, precision=highest, preferred_element_type=jnp.float32
+        )
+        work[size:, span] = done[size:]
+        return carry
+
+    lax.fori_loop(0, size // base, block, 0)
+
+
+def solve_kernel(
+    base_ref, high_ref, low_ref, lead_ref, gram_ref, out_ref, panel_ref,
+    panels, part, part_in, work, grid, side, send, recv, part_send, part_recv, side_send, side_recv, row_send, row_recv, row_own,
+):
     row = lax.axis_index("row")
     col = lax.axis_index("col")
     chip = col // 2
@@ -45,12 +336,59 @@
     sibling = (row, 2 * chip + 1 - core)
 
     barrier = pltpu.get_barrier_semaphore()
-    for step in range(1, CHIPS):
-        pl.semaphore_signal(
-            barrier, inc=1, device_id=(row, 2 * ((chip + step) % CHIPS) + core), device_id_type=MESH
-        )
-    pl.semaphore_signal(barrier, inc=1, device_id=sibling, device_id_type=MESH)
-    pl.semaphore_wait(barrier, CHIPS)
+    n_cols = lax.axis_size("col")
+    for step in range(1, n_cols):
+        pl.semaphore_signal(barrier, inc=1, device_id=(row, (col + step) % n_cols), device_id_type=MESH)
+    pl.semaphore_wait(barrier, n_cols - 1)
+    share = panel_ref.shape[0]
+
+    def swap():
+        return pltpu.make_async_remote_copy(
+            src_ref=gram_ref.at[pl.ds(pl.multiple_of((1 - core) * width, width), width)],
+            dst_ref=side,
+            send_sem=side_send,
+            recv_sem=side_recv,
+            device_id=sibling,
+            device_id_type=MESH,
+        )
+
+    def strip(m):
+        return work.at[pl.ds(2 * width + m * share, share)]
+
+    def hand_out(m):
+        return pltpu.make_async_remote_copy(
+            src_ref=strip(m),
+            dst_ref=panel_ref,
+            send_sem=row_send.at[m],
+            recv_sem=row_recv,
+            device_id=(row, CHIPS * core + m),
+            device_id_type=MESH,
+        )
+
+    def leading():
+        work[pl.ds(0, 2 * width)] = lead_ref[...]
+        own = pl.ds(pl.multiple_of(core * width, width), width)
+        other = pl.ds(pl.multiple_of((1 - core) * width, width), width)
+        tail = pl.ds(2 * width, width)
+        work[tail, own] = gram_ref[own]
+        swap().wait_recv()
+        work[tail, other] = side[...]
+        panel_solve(work, grid, 2 * width)
+        for m in range(CHIPS):
+            if m:
+                hand_out(m).start()
+            else:
+                pl.when(core == 1)(lambda: hand_out(0).start())
+                pl.when(core == 0)(lambda: pltpu.make_async_copy(strip(0), panel_ref, row_own).start())
+
+    def leading_sent():
+        swap().wait_send()
+        for m in range(CHIPS):
+            if m:
+                hand_out(m).wait_send()
+            else:
+                pl.when(core == 1)(lambda: hand_out(0).wait_send())
+                pl.when(core == 0)(lambda: pltpu.make_async_copy(strip(0), panel_ref, row_own).wait())
 
     def run(me):
         onward = [[b for a, b in ROUTES[j] if a == me] for j in range(CHIPS)]
@@ -123,7 +461,11 @@
                 finish(tick)
             return carry
 
+        if me == 0:
+            swap().start()
         lax.fori_loop(0, CHUNKS + lag, step, 0)
+        if me == 0:
+            leading()
 
         def drain(t, carry):
             exchange(t).wait_send()
@@ -132,12 +474,15 @@
             return carry
 
         lax.fori_loop(0, CHUNKS, drain, 0)
+        if me == 0:
+            leading_sent()
 
     for me in range(CHIPS):
         pl.when(chip == me)(functools.partial(run, me))
-
-
-def solve(iterate, factor, inverses):
+    pl.when(col > 0)(lambda: hand_out(0).wait_recv())
+
+
+def solve(iterate, factor, inverses, lead, gram_block):
     n_rows, width = iterate.shape
     order, _ = factor.shape
     rows = n_rows // CHUNKS
@@ -160,71 +505,40 @@
     vmem = pl.BlockSpec(memory_space=pltpu.VMEM)
     return pl.pallas_call(
         solve_kernel,
-        out_shape=jax.ShapeDtypeStruct((n_rows, width), jnp.float32),
-        in_specs=[vmem] * 3,
-        out_specs=vmem,
+        out_shape=(
+            jax.ShapeDtypeStruct((n_rows, width), jnp.float32),
+            jax.ShapeDtypeStruct((width // CHIPS, 2 * width), jnp.float32),
+        ),
+        in_specs=[vmem] * 5,
+        out_specs=(vmem, vmem),
         scratch_shapes=[
             pltpu.VMEM((CHIPS - 1, n_rows, width), jnp.float32),
             pltpu.VMEM((CHUNKS, 2, rows, width), jnp.float32),
             pltpu.VMEM((CHUNKS, rows, width), jnp.float32),
+            pltpu.VMEM((3 * width, 2 * width), jnp.float32),
+            pltpu.VMEM((width // 2, width), jnp.float32),
+            pltpu.VMEM((width, width), jnp.float32),
             pltpu.SemaphoreType.DMA((SLOTS, CHUNKS)),
             pltpu.SemaphoreType.DMA((CHIPS, CHUNKS)),
             pltpu.SemaphoreType.DMA((CHUNKS,)),
             pltpu.SemaphoreType.DMA((CHUNKS,)),
+            pltpu.SemaphoreType.DMA,
+            pltpu.SemaphoreType.DMA,
+            pltpu.SemaphoreType.DMA((CHIPS,)),
+            pltpu.SemaphoreType.DMA,
+            pltpu.SemaphoreType.DMA,
         ],
         compiler_params=pltpu.CompilerParams(
             collective_id=0, has_side_effects=True, vmem_limit_bytes=40 << 20
         ),
         cost_estimate=pl.CostEstimate(flops=3 * 10**9, bytes_accessed=10**7, transcendentals=0),
-    )(base, w_high, w_low)
-
-
-def from_root(block, axis, source):
-    block = jnp.where(lax.axis_index(axis) == source, block, jnp.zeros_like(block))
-    return lax.psum(block, axis)
+    )(base, w_high, w_low, lead, gram_block)
 
 
 def on_device(iterate, factor, inverses):
-    highest = lax.Precision.HIGHEST
-    row_dev, local_width = iterate.shape
-    n_rows = lax.axis_size("row")
-    n_cols = lax.axis_size("col")
-    full_order = local_width * n_cols
-    panel_width = inverses.shape[1]
-    panels = inverses.shape[0]
-    owners = panel_width // local_width
-    row_index = lax.axis_index("row")
-    col_index = lax.axis_index("col")
-    scale_factor = 3.0 / (row_dev * n_rows)
-    block_rows = full_order // n_rows
-    gathered = lax.all_gather(iterate, "col", axis=1, tiled=True)
-    summed = lax.psum_scatter(
-        lax.dot_general(
-            gathered,
-            iterate,
-            (((0,), (0,)), ((), ())),
-            precision=highest,
-            preferred_element_type=jnp.float32,
-        ),
-        "row",
-        scatter_dimension=0,
-        tiled=True,
-    )
-    row_ids = row_index * block_rows + jnp.arange(block_rows)[:, None]
-    col_ids = col_index * local_width + jnp.arange(local_width)[None, :]
-    gram_block = jnp.where(row_ids == col_ids, 1.0, 0.0).astype(jnp.float32) + scale_factor * summed
-    offset = jnp.minimum(col_index * local_width, panel_width - local_width)
-    empty = jnp.zeros((block_rows, panel_width), jnp.float32)
-    placed = lax.dynamic_update_slice_in_dim(empty, gram_block, offset, 1)
-    placed = jnp.where(col_index < owners, placed, 0.0)
-    panel_rows = lax.psum(placed, "col")
-    leading_rows = from_root(panel_rows, "row", 0)
-    leading = jnp.linalg.cholesky(leading_rows)
-    share_rows = block_rows // n_cols
-    my_rows = lax.dynamic_slice_in_dim(panel_rows, col_index * share_rows, share_rows, 0)
-    panel_factor = jax.scipy.linalg.solve_triangular(leading, my_rows.T, lower=True).T
-    solved = solve(iterate, factor, inverses)
-    return (gram_block, panel_factor, solved)
+    gram_block, lead = gram(iterate)
+    solved, panel = solve(iterate, factor, inverses, lead, gram_block)
+    return (gram_block, panel, solved)
 
 
 def solution(mesh):

time: 575 us -> 231 us (0.40)
  waiting for transfers between devices: 271 us -> 0.01 us
  other arithmetic: 127 us -> 0 us
  Pallas kernels: 97.4 us -> 212 us
  matrix products: 28.8 us -> 9.12 us
  local copies, waits for them, and re-layouts: 25.6 us -> 6.94 us
  between operations: 17.1 us -> 0.71 us
    another operation x17 -> x0, other arithmetic: 121 us -> none  [the longest x14 80.9 us: on_device(): leading = jnp.linalg.cholesky(leading_rows)]
    psum x2 -> x0, waiting for transfers between devices: 115 us -> none  [the longest x1 115 us: on_device(): panel_rows = lax.psum(placed, 'col')]
    pallas_call x1 -> x2, Pallas kernels: 97.4 us -> 212 us  [the longest x1 111 us: solve(): pl.pallas_call(solve_kernel, out_shape=(jax.ShapeDtypeStruct((n_rows, wid...]
    reduce_scatter x1 -> x0, waiting for transfers between devices: 80.7 us -> none  [on_device(): lax.psum_scatter(lax.dot_general(gathered, iterate, (((0,), (0,)), ((), (...]
    all_gather x1 -> x0, waiting for transfers between devices: 75.1 us -> none  [on_device(): gathered = lax.all_gather(iterate, 'col', axis=1, tiled=True)]
    dot_general x1 -> x0, matrix products: 15.6 us -> none  [on_device(): lax.dot_general(gathered, iterate, (((0,), (0,)), ((), ())), precision=hi...]
    another operation x35 -> x0, local copies, waits for them, and re-layouts: 15 us -> none
  transfers between devices with their start and end apart: 5 -> 1, of which waited for: 3 -> 0; matrix products, arithmetic and copies ran while one was open for 3% -> 1% of each run, Pallas kernels for 17% -> 44%
where the time goes in v3:
time: 231 us; the launch traced here: 229 us
  Pallas kernels  212 us (92%)
  matrix products  9.12 us (4%)
  local copies, waits for them, and re-layouts  6.94 us (3%)
    pallas_call x1, Pallas kernels, solve(): pl.pallas_call(solve_kernel, out_shape=(jax.ShapeDtypeStruct((n_rows, wid...  111 us
    pallas_call x1, Pallas kernels, gram(): pl.pallas_call(gram_kernel, out_shape=(jax.ShapeDtypeStruct((2 * width, w...  101 us
    dot_general x1, matrix products, solve(): jnp.dot(both, inverse, precision=high, preferred_element_type=jnp.float32)  7.24 us
    dynamic_slice x1, local copies, waits for them, and re-layouts, solve(): lax.dynamic_index_in_dim(blocks, core, 1, keepdims=False)  4.63 us
  transfers between devices with their start and end apart: 1, of which 0 were waited for; matrix products, arithmetic and copies ran while one was open for 1% of the time, Pallas kernels for 44%

profile of v3, /device:TPU:14, one launch (start us, length us, event | category | flops | bytes accessed | tf_op | source)
XLA Modules:
  0.0 228.7 jit_solution(1053339616368167436)
XLA Ops:
  0.7 0.0 copy-start
  0.7 4.6 %constant_dynamic-slice_fusion.1 = (f32[8,1,256,256]{3,2,1,0:T(8,128)}, f32[8,1,256,256]{3,2,1,0:T(8,128)}) fusion(f32[8,2,256,256]{3,2,1,0:T(8,128)} %bitcast.14, s32[]{:T(128)S(6)} %select_n.44, s32[]{:T(128)S(6)} %select_n.45), kind=kLoop, calls=%fused_computation.18 | loop fusion | bytes 8388616 | tf_op jit(solution)/shard_map/jit(dynamic_index_in_dim)/dynamic_slice | solution.py:494
  5.3 0.0 collective-permute-start
  5.3 0.0 copy-done
  5.3 101.3 %shard_map.58 = (f32[512,256]{1,0:T(8,128)S(1)}, f32[512,512]{1,0:T(8,128)S(1)}) custom-call(f32[768,256]{1,0:T(8,128)S(1)} %copy-done), custom_call_target="tpu_custom_call" | custom-call | flops 5000000000 | bytes 10000000 | tf_op jit(solution)/shard_map/pallas_call | solution.py:240
  106.6 1.9 convolution_bitcast_fusion.base_ref
  108.5 0.0 collective-permute-done
  108.5 7.2 %fusion = (bf16[2048,512]{1,0:T(8,128)(2,1)S(1)}, bf16[2048,512]{1,0:T(8,128)(2,1)S(1)}) fusion(f32[8,512,512]{2,1,0:T(8,128)} %param.5, s32[]{:T(128)S(6)} %select_n.38, f32[2048,256]{1,0:T(8,128)} %collective-permute-done, f32[2048,256]{1,0:T(8,128)} %bitcast.15, pred[]{:T(512)S(6)} %eq.5), kind=kOutput, calls=%fused_computation.2 | convolution fusion | flops 3228565504 | bytes 9437189 | tf_op jit(solution)/shard_map/dot_general | solution.py:499
  115.8 110.7 %shard_map.59 = (f32[768,256]{1,0:T(8,128)S(1)}, f32[32,512]{1,0:T(8,128)S(1)}) custom-call(f32[768,512]{1,0:T(8,128)S(1)} %convolution_bitcast_fusion.base_ref, bf16[2048,512]{1,0:T(8,128)(2,1)S(1)} %get-tuple-element.12.high_ref, bf16[2048,512]{1,0:T(8,128)(2,1)S(1)} %get-tuple-element.11.low_ref, f32[512,512]{1,0:T(8,128)S(1)} %get-tuple-element.8.lead_ref, ...), custom_call_target="tpu_custom_call" | custom-call | flops 3000000000 | bytes 10000000 | tf_op jit(solution)/shard_map/pallas_call | solution.py:506
  226.4 0.8 copy.11
  227.2 0.6 copy.12
  227.9 0.9 copy.13
Async XLA Ops:
  0.7 4.6 %copy-start = (f32[768,256]{1,0:T(8,128)S(1)}, f32[768,256]{1,0:T(8,128)}, u32[]{:S(2)}) copy-start(f32[768,256]{1,0:T(8,128)} %mine_ref.1) | copy-start | bytes 2359300
  5.3 103.2 %collective-permute-start = (f32[2048,256]{1,0:T(8,128)}, f32[2048,256]{1,0:T(8,128)}, u32[]{:S(2)}, u32[]{:S(2)}) collective-permute-start(f32[2048,256]{1,0:T(8,128)} %bitcast.4), channel_id=1, source_target_pairs={{0,1},{1,0},{2,3},{3,2},{4,5},{5,4},{6,7},{7,6},{8,9},{9,8},{10,11... | collective-permute-start | bytes 6291464 | tf_op jit(solution)/shard_map/ppermute | solution.py:497

commit v4 on v0

v4 whole, which is shorter than its diff:
```python
import functools
import types

import jax
import jax.numpy as jnp
from jax import lax
from jax.experimental import pallas as pl
from jax.experimental.pallas import tpu as pltpu
from jax.sharding import PartitionSpec as P

CHIPS = 8
RING = 4
MESH = pl.DeviceIdType.MESH


def split(value):
    high = value.astype(jnp.bfloat16)
    return high, (value - high.astype(jnp.float32)).astype(jnp.bfloat16)


def dot3(left, right):
    dot = functools.partial(jnp.dot, preferred_element_type=jnp.float32)
    return dot(left[0], right[0]) + (dot(left[0], right[1]) + dot(left[1], right[0]))


def dot3_turned(left, right):
    dot = functools.partial(
        lax.dot_general, dimension_numbers=(((0,), (0,)), ((), ())), preferred_element_type=jnp.float32
    )
    return dot(left[0], right[0]) + (dot(left[0], right[1]) + dot(left[1], right[0]))


def dot_exact_turned(left, right):
    return lax.dot_general(
        left, right, (((1,), (1,)), ((), ())), precision=lax.Precision.HIGHEST, preferred_element_type=jnp.float32
    )


def factor_block(grid):
    base = grid.shape[0]
    for p in range(base // 8):
        rows = slice(8 * p, 8 * p + 8)
        panel = grid[rows]
        sub = lax.broadcasted_iota(jnp.int32, panel.shape, 0)
        columns = [jnp.broadcast_to(panel[:, 8 * p + c : 8 * p + c + 1], panel.shape) for c in range(8)]
        scales = jnp.zeros_like(panel)
        for j in range(8):
            pivot = jnp.broadcast_to(columns[j][j : j + 1], panel.shape)
            guess = lax.rsqrt(pivot)
            guess = guess * (1.5 - 0.5 * pivot * guess * guess)
            below = jnp.where(sub > j, columns[j] * (guess * guess), 0.0)
            scales = jnp.where(sub == j, guess, scales)
            for c in range(j + 1, 8):
                columns[c] = columns[c] - below * columns[c][j : j + 1]
            panel = panel - below * panel[j : j + 1]
        panel = panel * scales
        grid[rows] = panel
        if 8 * p + 8 < base:
            rest = slice(8 * p + 8, base)
            turned = panel[:, :base].T[8 * p + 8 :]
            value = grid[rest]
            for j in range(8):
                value = value - turned[:, j : j + 1] * panel[j : j + 1]
            grid[rest] = value


def factor_step(work, grid, inverted, below, s):
    base = grid.shape[0]
    span = pl.ds(pl.multiple_of(s * base, base), base)
    shape = (base, base)
    eye = lax.broadcasted_iota(jnp.int32, shape, 0) == lax.broadcasted_iota(jnp.int32, shape, 1)
    grid[:, :base] = work[span, span]
    grid[:, base:] = jnp.where(eye, 1.0, 0.0)
    factor_block(grid)
    inverted[s] = grid[:, base:]
    done = dot_exact_turned(work[:, span], grid[:, base:])
    later = lax.broadcasted_iota(jnp.int32, done.shape, 0) >= (s + 1) * base
    done = jnp.where(later, done, 0.0)
    below[s] = done
    work[...] = work[...] - dot_exact_turned(done, done)


def solve_rows(rows_ref, inverted, below):
    blocks, base, _ = inverted.shape

    def step(s, carry):
        span = pl.ds(pl.multiple_of(s * base, base), base)
        done = dot_exact_turned(rows_ref[:, span], inverted[s])
        rows_ref[...] = rows_ref[...] - dot_exact_turned(done, below[s])
        rows_ref[:, span] = done
        return carry

    lax.fori_loop(0, blocks, step, 0)


def scratch_shapes(n, width, n_rows):
    f32, bf16 = jnp.float32, jnp.bfloat16
    vmem, dma = pltpu.VMEM, pltpu.SemaphoreType.DMA
    z_rows = width // RING
    return dict(
        theirs=vmem((n, width), f32),
        got=vmem((CHIPS, n, width), f32),
        high=vmem((2, n, width), bf16),
        low=vmem((2, n, width), bf16),
        prod=vmem((CHIPS, 2, width, width), f32),
        land=vmem((n_rows, 2, width, width), f32),
        slices=vmem((n_rows, 2, width // n_rows, width), f32),
        work=vmem((2 * width, 2 * width), f32),
        grid=vmem((width // 2, width), f32),
        inverted=vmem((4, width // 2, width // 2), f32),
        below=vmem((4, 2 * width, width // 2), f32),
        lead_in=vmem((2 * width, 2 * width), f32),
        first=vmem((width, 2 * width), f32),
        side=vmem((width, width), f32),
        their_factor=vmem((CHIPS, width, width), f32),
        inverse=vmem((2, width, 2 * width), f32),
        inverse_high=vmem((2, width, 2 * width), bf16),
        inverse_low=vmem((2, width, 2 * width), bf16),
        starts=vmem((CHIPS, 2, z_rows, width), f32),
        w_high=vmem((CHIPS - 1, width, 2 * width), bf16),
        w_low=vmem((CHIPS - 1, width, 2 * width), bf16),
        chain=vmem((CHIPS - 1, CHIPS - 1, 2, z_rows, width), f32),
        part=vmem((CHIPS, 2, 2, z_rows, width), f32),
        part_in=vmem((CHIPS, 2, z_rows, width), f32),
        own=vmem((CHIPS - 1, 2, z_rows, width), f32),
        cols=vmem((CHIPS - 1, 2, width, width), f32),
        total=vmem((2, n, width), f32),
        total_in=vmem((n, width), f32),
        send=dma((9,)),
        recv=dma((9,)),
        push=dma((CHIPS, 2)),
        landed=dma((n_rows, 2)),
        cut=dma((n_rows,)),
        cut_in=dma((n_rows,)),
        share=dma((n_rows, 2)),
        shared=dma((n_rows, 2)),
        local=dma((3,)),
        factor_send=dma,
        factor_recv=dma,
        part_send=dma((CHIPS,)),
        part_recv=dma((CHIPS,)),
        chain_send=dma((CHIPS, CHIPS)),
        chain_recv=dma((CHIPS, CHIPS)),
        col_send=dma((CHIPS, 5)),
        col_relay=dma((CHIPS, 2, 2)),
        col_recv=dma((CHIPS, 5, 2)),
        total_send=dma,
        total_recv=dma,
        side_send=dma,
        side_recv=dma,
        row_send=dma((CHIPS,)),
        row_recv=dma,
    )


def fused_kernel(names, mine_ref, factor_ref, inverses_ref, gram_ref, panel_ref, solved_ref, *scratch):
    v = types.SimpleNamespace(**dict(zip(names, scratch)))
    row = lax.axis_index("row")
    col = lax.axis_index("col")
    n_rows = lax.axis_size("row")
    n_cols = lax.axis_size("col")
    chip = col // 2
    core = col % 2
    x, y = chip % 4, chip // 4
    z, plane = row % RING, row // RING
    n, width = mine_ref.shape
    half = n // 2
    piece = width // n_rows
    z_rows = width // RING
    scale = 3.0 / (n * n_rows)
    sibling = (row, 2 * chip + 1 - core)

    barrier = pltpu.get_barrier_semaphore()
    for step in range(1, n_cols):
        pl.semaphore_signal(barrier, inc=1, device_id=(row, (col + step) % n_cols), device_id_type=MESH)
    for step in range(1, n_rows):
        for other in range(2):
            pl.semaphore_signal(
                barrier, inc=1, device_id=((row + step) % n_rows, 2 * chip + other), device_id_type=MESH
            )
    pl.semaphore_wait(barrier, n_cols - 1 + 2 * (n_rows - 1))

    def copy(source, target, out, arrival, device):
        return pltpu.make_async_remote_copy(
            src_ref=source, dst_ref=target, send_sem=out, recv_sem=arrival, device_id=device, device_id_type=MESH
        )

    def at(dx, dy):
        return 4 * ((y + dy) % 2) + (x + dx) % 4

    left, right, partner, far = at(3, 0), at(1, 0), at(0, 1), at(2, 0)
    top, low_half = pl.ds(0, half), pl.ds(half, half)
    at_right, at_left = (row, 2 * right + core), (row, 2 * left + core)
    at_partner = (row, 2 * partner + core)
    got = v.got
    sends = [
        copy(mine_ref, v.theirs, v.send.at[8], v.recv.at[8], sibling),
        copy(mine_ref, got.at[chip], v.send.at[0], v.recv.at[0], at_right),
        copy(mine_ref, got.at[chip], v.send.at[1], v.recv.at[1], at_left),
        copy(mine_ref, got.at[chip], v.send.at[2], v.recv.at[2], at_partner),
        copy(got.at[left, top], got.at[left, top], v.send.at[3], v.recv.at[3], at_right),
        copy(got.at[right, low_half], got.at[right, low_half], v.send.at[4], v.recv.at[4], at_left),
        copy(got.at[partner], got.at[partner], v.send.at[5], v.recv.at[5], at_right),
        copy(got.at[partner], got.at[partner], v.send.at[6], v.recv.at[6], at_left),
        copy(got.at[far], got.at[far], v.send.at[7], v.recv.at[7], at_partner),
    ]
    give_factor = copy(factor_ref.at[:, 1 - core], v.their_factor, v.factor_send, v.factor_recv, sibling)
    own_span = pl.ds(pl.multiple_of(core * width, width), width)
    fetch = [
        pltpu.make_async_copy(inverses_ref.at[chip, 0], v.inverse.at[0], v.local.at[0]),
        pltpu.make_async_copy(inverses_ref.at[chip, 1], v.inverse.at[1], v.local.at[1]),
        pltpu.make_async_copy(
            inverses_ref.at[:, :, pl.ds(pl.multiple_of(z * z_rows, z_rows), z_rows), own_span], v.starts, v.local.at[2]
        ),
    ]
    for one in sends[:4]:
        one.start()
    give_factor.start()
    for one in fetch:
        one.start()
    got[chip] = mine_ref[...]
    own_high, own_low = split(mine_ref[...])
    v.high[core] = own_high
    v.low[core] = own_low
    sends[0].wait_recv()
    their_high, their_low = split(v.theirs[...])
    v.high[1 - core] = their_high
    v.low[1 - core] = their_low

    def order(idx):
        dx = jnp.where(
            (idx == 1) | (idx == 5), 3, jnp.where((idx == 2) | (idx == 6), 1, jnp.where((idx == 4) | (idx == 7), 2, 0))
        )
        dy = jnp.where((idx == 3) | (idx > 4), 1, 0)
        return at(dx, dy)

    def away(block, to):
        return copy(
            v.prod.at[block, to],
            v.land.at[row, core],
            v.push.at[block, to],
            v.landed.at[row, core],
            (block, 2 * chip + to),
        )

    def product(idx):
        block = order(idx)
        lefts = split(got[block])
        for to in range(2):
            v.prod[block, to] = dot3_turned(lefts, (v.high[to], v.low[to]))

        @pl.when(block != row)
        def _():
            away(block, core).start()

        @pl.when(block == row)
        def _():
            v.land[row, core] = v.prod[block, core]

        away(block, 1 - core).start()

    def slice_to(other):
        return copy(
            v.prod.at[0, :, pl.ds(pl.multiple_of(other * piece, piece), piece)],
            v.slices.at[row],
            v.cut.at[other],
            v.cut_in.at[row],
            (other, core),
        )

    def lead_rows(at_row, at_core):
        return v.lead_in.at[pl.ds(pl.multiple_of(at_core * width + at_row * piece, piece), piece)]

    def share_to(step, to):
        rows = lead_rows(row, core)
        return copy(rows, rows, v.share.at[step, to], v.shared.at[row, core], ((row + step) % n_rows, to))

    def lead_slices():
        for step in range(1, n_rows):
            slice_to((row + step) % n_rows).start()
        v.slices[row] = v.prod[0, :, pl.ds(pl.multiple_of(row * piece, piece), piece)]
        for step in range(1, n_rows):
            source = (row + step) % n_rows
            copy(
                v.slices.at[row], v.slices.at[source], v.cut.at[source], v.cut_in.at[source], (source, core)
            ).wait_recv()
        total = v.slices[0]
        for other in range(1, n_rows):
            total = total + v.slices[other]
        whole = scale * jnp.concatenate([total[0], total[1]], axis=1)
        first = core * width + row * piece
        shape = (piece, 2 * width)
        there = lax.broadcasted_iota(jnp.int32, shape, 0) + first == lax.broadcasted_iota(jnp.int32, shape, 1)
        lead_rows(row, core)[...] = whole + jnp.where(there, 1.0, 0.0)
        for step in range(1, n_rows):
            for to in range(2):
                share_to(step, to).start()
        share_to(0, 1 - core).start()

    def lead_wait():
        for step in range(n_rows):
            for other in range(2):
                source = (row + step) % n_rows

                @pl.when((step > 0) | (core != other))
                def _():
                    rows = lead_rows(source, other)
                    copy(rows, rows, v.share.at[0, 0], v.shared.at[source, other], (source, 0)).wait_recv()

        v.work[...] = v.lead_in[...]

    def couple(j):
        pairs = [(v.inverse_high[side], v.inverse_low[side]) for side in (core, 1 - core)]
        value = dot3(split(factor_ref[j, core]), pairs[0]) + dot3(split(v.their_factor[j]), pairs[1])
        w_high, w_low = split(value)
        v.w_high[j] = w_high
        v.w_low[j] = w_low

    def trade(d):
        return copy(v.part.at[d, 1 - core], v.part_in.at[d], v.part_send.at[d], v.part_recv.at[d], sibling)

    def along(i, j, target):
        return copy(
            v.own.at[i], v.chain.at[i, j], v.chain_send.at[i, target], v.chain_recv.at[i, j], (row, 2 * target + core)
        )

    def z_span(at_z, start=0, size=z_rows):
        return pl.ds(pl.multiple_of(at_z * z_rows + start, size), size)

    def z_device(step, to):
        return (RING * plane + (z + step) % RING, 2 * chip + to)

    def spread(i):
        place = v.cols.at[i, core, z_span(z)]
        copies = [copy(v.own.at[i, 1 - core], place, v.col_send.at[i, 0], v.col_recv.at[i, 0, core], sibling)]
        for slot, step in ((1, 1), (2, RING - 1)):
            for to in range(2):
                copies.append(
                    copy(
                        v.own.at[i, to],
                        place,
                        v.col_send.at[i, 2 * slot - 1 + to],
                        v.col_recv.at[i, slot, core],
                        z_device(step, to),
                    )
                )
        return copies

    def onward(i, side, slot):
        step, start = ((1, 0), (RING - 1, z_rows // 2))[slot - 1]
        place = v.cols.at[i, side, z_span((z - step) % RING, start, z_rows // 2)]
        return copy(
            place, place, v.col_relay.at[i, side, slot - 1], v.col_recv.at[i, slot + 2, side], z_device(step, core)
        )

    def arrived(i, side, slot):
        rows = z_span(z) if slot < 3 else z_span(z, 0, z_rows // 2)
        place = v.cols.at[i, side, rows]
        return copy(place, place, v.col_send.at[i, 0], v.col_recv.at[i, slot, side], sibling)

    def chain_step(d):
        i = chip - d

        def term(left, j):
            left = left.reshape(2 * z_rows, width)
            return dot3(split(left), (v.w_high[j], v.w_low[j])).reshape(2, z_rows, 2 * width)

        def add(value):
            for side in range(2):
                v.part[d, side] = v.part[d, side] + value[:, :, side * width : (side + 1) * width]

        value = term(v.starts[i], i)
        for side in range(2):
            v.part[d, side] = value[:, :, side * width : (side + 1) * width]

        def more(j, carry):
            copy(v.own.at[i], v.chain.at[i, j], v.chain_send.at[i, 0], v.chain_recv.at[i, j], sibling).wait_recv()
            add(term(v.chain[i, j], j))
            return carry

        lax.fori_loop(i + 1, chip, more, 0)
        trade(d).start()
        trade(d).wait_recv()
        v.own[i] = -(v.part[d, core] + v.part_in[d])

        def tell(target, carry):
            along(i, chip, target).start()
            return carry

        lax.fori_loop(chip + 1, CHIPS, tell, 0)
        for one in spread(i):
            one.start()
        v.cols[i, core, z_span(z)] = v.own[i, core]
        pl.when(i > 0)(lambda: couple(i - 1))

    def relay(i):
        for side in range(2):
            for slot in (1, 2):
                arrived(i, side, slot).wait_recv()
                onward(i, side, slot).start()

    for one in fetch:
        one.wait()
    for side in range(2):
        high, low = split(v.inverse[side])
        v.inverse_high[side] = high
        v.inverse_low[side] = low

    def body(idx, carry):
        @pl.when(idx == 1)
        def _():
            for one in sends[1:4]:
                one.wait_recv()
            for one in sends[4:8]:
                one.start()

        @pl.when(idx == 4)
        def _():
            sends[4].wait_recv()
            sends[5].wait_recv()
            sends[8].start()

        @pl.when(idx > 4)
        def _():
            copy(mine_ref, got.at[chip], v.send.at[0], v.recv.at[idx], at_right).wait_recv()

        product(idx)

        @pl.when(idx == 0)
        def _():
            pl.when(chip == 0)(lead_slices)
            give_factor.wait_recv()
            pl.when(chip > 0)(lambda: couple(chip - 1))

        pl.when((idx < CHIPS - 1) & (chip > idx))(lambda: chain_step(idx + 1))
        pl.when((idx > 0) & (chip >= idx))(lambda: relay(chip - idx))

        @pl.when((idx >= 4) & (chip == 0))
        def _():
            pl.when(idx == 4)(lead_wait)
            factor_step(v.work, v.grid, v.inverted, v.below, idx - 4)

        return carry

    lax.fori_loop(0, CHIPS, body, 0)

    lefts = split(got[chip])
    for side in range(2):
        span = slice(side * width, (side + 1) * width)
        v.total[side] = dot3(lefts, (v.inverse_high[core, :, span], v.inverse_low[core, :, span]))

    def accumulate(step, carry):
        i = chip - 1 - step
        arrived(i, 1 - core, 0).wait_recv()
        for side in range(2):
            for slot in (3, 4):
                arrived(i, side, slot).wait_recv()
        lefts = split(got[i])
        for side in range(2):
            v.total[side] = v.total[side] + dot3(lefts, split(v.cols[i, side]))
        return carry

    lax.fori_loop(0, chip, accumulate, 0)
    give_total = copy(v.total.at[1 - core], v.total_in, v.total_send, v.total_recv, sibling)
    give_total.start()

    for other in range(2):
        for step in range(n_rows):
            source = (row + step) % n_rows

            @pl.when((step > 0) | (core != other))
            def _():
                copy(
                    v.prod.at[0, 0], v.land.at[source, other], v.push.at[0, 0], v.landed.at[source, other], sibling
                ).wait_recv()

        total = v.land[0, other]
        for source in range(1, n_rows):
            total = total + v.land[source, other]
        shape = (width, width)
        shift = (row * 2 + other - (2 * chip + core)) * width
        there = lax.broadcasted_iota(jnp.int32, shape, 0) + shift == lax.broadcasted_iota(jnp.int32, shape, 1)
        gram_ref[pl.ds(other * width, width)] = jnp.where(there, 1.0, 0.0) + scale * total

    share = panel_ref.shape[0]
    other_span = pl.ds(pl.multiple_of((1 - core) * width, width), width)
    swap = copy(gram_ref.at[other_span], v.side, v.side_send, v.side_recv, sibling)

    def hand_out(m):
        return copy(
            v.first.at[pl.ds(m * share, share)], panel_ref, v.row_send.at[m], v.row_recv, (row, CHIPS * core + m)
        )

    @pl.when(chip == 0)
    def _():
        swap.start()
        v.first[:, own_span] = gram_ref[own_span]
        swap.wait_recv()
        v.first[:, other_span] = v.side[...]
        solve_rows(v.first, v.inverted, v.below)
        for m in range(1, CHIPS):
            hand_out(m).start()
        pl.when(core == 1)(lambda: hand_out(0).start())

        @pl.when(core == 0)
        def _():
            panel_ref[...] = v.first[pl.ds(0, share)]

    give_total.wait_recv()
    solved_ref[...] = v.total[core] + v.total_in[...]
    pl.when(col > 0)(lambda: hand_out(0).wait_recv())

    @pl.when(chip == 0)
    def _():
        for step in range(1, n_rows):
            slice_to((row + step) % n_rows).wait_send()
            for to in range(2):
                share_to(step, to).wait_send()
        share_to(0, 1 - core).wait_send()
        swap.wait_send()
        for m in range(1, CHIPS):
            hand_out(m).wait_send()
        pl.when(core == 1)(lambda: hand_out(0).wait_send())

    for one in sends:
        one.wait_send()
    give_factor.wait_send()
    give_total.wait_send()

    def drain_push(block, carry):
        pl.when(block != row)(lambda: away(block, core).wait_send())
        away(block, 1 - core).wait_send()
        return carry

    lax.fori_loop(0, CHIPS, drain_push, 0)

    def drain_chain(i, carry):
        trade(chip - i).wait_send()

        def told(target, carry):
            along(i, chip, target).wait_send()
            return carry

        lax.fori_loop(chip + 1, CHIPS, told, 0)
        for one in spread(i):
            one.wait_send()
        for side in range(2):
            for slot in (1, 2):
                onward(i, side, slot).wait_send()
        return carry

    lax.fori_loop(0, chip, drain_chain, 0)


def on_device(iterate, factor, inverses):
    n, width = iterate.shape
    n_rows = lax.axis_size("row")
    n_cols = lax.axis_size("col")
    vmem = pl.BlockSpec(memory_space=pltpu.VMEM)
    scratch = scratch_shapes(n, width, n_rows)
    return pl.pallas_call(
        functools.partial(fused_kernel, tuple(scratch)),
        out_shape=(
            jax.ShapeDtypeStruct((2 * width, width), jnp.float32),
            jax.ShapeDtypeStruct((2 * width // n_cols, 2 * width), jnp.float32),
            jax.ShapeDtypeStruct((n, width), jnp.float32),
        ),
        in_specs=[vmem, vmem, pl.BlockSpec(memory_space=pl.ANY)],
        out_specs=(vmem, vmem, vmem),
        scratch_shapes=list(scratch.values()),
        compiler_params=pltpu.CompilerParams(
            collective_id=0, has_side_effects=True, vmem_limit_bytes=60 << 20
        ),
        cost_estimate=pl.CostEstimate(flops=10**10, bytes_accessed=2 * 10**7, transcendentals=0),
    )(iterate, factor.reshape(CHIPS, 2, width, width), inverses.reshape(CHIPS, 2, width, 2 * width))


def solution(mesh):
    placed = (P("row", "col"), P(None, "col"), P())
    return jax.shard_map(
        on_device,
        mesh=mesh,
        in_specs=placed,
        out_specs=(P("row", "col"), P(("row", "col"), None), P("row", "col")),
        check_vma=False,
    )
```

time: 1460 us -> 190 us (0.13)
  the two profiles are of different devices: /device:TPU:14 before, /device:TPU:47 now
where the time goes in v4:
time: 190 us; the launch traced here: 189 us
  Pallas kernels  183 us (96%)
  local copies, waits for them, and re-layouts  5.4 us (3%)
    pallas_call x1, Pallas kernels, on_device(): pl.pallas_call(functools.partial(fused_kernel, tuple(scratch)), out_shape...  183 us
    unnamed x3, local copies, waits for them, and re-layouts  5.4 us

profile of v4, /device:TPU:47, one launch (start us, length us, event | category | flops | bytes accessed | tf_op | source)
XLA Modules:
  0.0 189.3 jit_solution(4888313465319092540)
XLA Ops:
  0.6 183.2 %shard_map.58 = (f32[512,256]{1,0:T(8,128)}, f32[32,512]{1,0:T(8,128)}, f32[768,256]{1,0:T(8,128)}) custom-call(f32[768,256]{1,0:T(8,128)} %mine_ref.1, f32[8,2,256,256]{3,2,1,0:T(8,128)} %bitcast.3, f32[8,2,256,512]{3,2,1,0:T(8,128)} %bitcast.2), custom_call_target="tpu_custom_call" | custom-call | flops 10000000000 | bytes 20000000 | tf_op jit(solution)/shard_map/pallas_call | solution.py:561
  183.9 1.9 copy.9
  185.7 1.5 copy.10
  187.2 2.1 %copy.11 = f32[768,256]{1,0:T(8,128)} copy(f32[768,256]{1,0:T(8,128)} %get-tuple-element.8) | data formatting | bytes 1572864

commit v5 on v4

--- a/solution.py
+++ b/solution.py
@@ -103,7 +103,11 @@
         high=vmem((2, n, width), bf16),
         low=vmem((2, n, width), bf16),
         prod=vmem((CHIPS, 2, width, width), f32),
-        land=vmem((n_rows, 2, width, width), f32),
+        hop=vmem((CHIPS, width, width), f32),
+        land=vmem((2, 2, 2, width, width), f32),
+        beside=vmem((2, width, width), f32),
+        cross=vmem((2, width, width), f32),
+        cross_in=vmem((2, width, width), f32),
         slices=vmem((n_rows, 2, width // n_rows, width), f32),
         work=vmem((2 * width, 2 * width), f32),
         grid=vmem((width // 2, width), f32),
@@ -129,7 +133,12 @@
         send=dma((9,)),
         recv=dma((9,)),
         push=dma((CHIPS, 2)),
-        landed=dma((n_rows, 2)),
+        hop_send=dma((CHIPS, 2)),
+        hop_recv=dma((CHIPS,)),
+        landed=dma((2, 2, 2)),
+        beside_recv=dma((2,)),
+        cross_send=dma((2,)),
+        cross_recv=dma((2,)),
         cut=dma((n_rows,)),
         cut_in=dma((n_rows,)),
         share=dma((n_rows, 2)),
@@ -234,13 +243,35 @@
         dy = jnp.where((idx == 3) | (idx > 4), 1, 0)
         return at(dx, dy)
 
-    def away(block, to):
+    def ahead(block):
+        return (block % RING - z + RING) % RING
+
+    def z_peer(step, to):
+        return (RING * plane + (z + step) % RING, 2 * chip + to)
+
+    def hop_to(block, side):
+        step = (1, RING - 1)[side]
+        return copy(
+            v.prod.at[block, side], v.hop.at[block], v.hop_send.at[block, side], v.hop_recv.at[block], z_peer(step, core)
+        )
+
+    def away(block, side, to):
+        step = (1, RING - 1)[side]
         return copy(
             v.prod.at[block, to],
-            v.land.at[row, core],
+            v.land.at[side, block // RING, core],
             v.push.at[block, to],
-            v.landed.at[row, core],
-            (block, 2 * chip + to),
+            v.landed.at[side, block // RING, core],
+            z_peer(step, to),
+        )
+
+    def hand_beside(block):
+        return copy(
+            v.prod.at[block, 1 - core],
+            v.beside.at[block // RING],
+            v.push.at[block, 1 - core],
+            v.beside_recv.at[block // RING],
+            sibling,
         )
 
     def product(idx):
@@ -248,16 +279,52 @@
         lefts = split(got[block])
         for to in range(2):
             v.prod[block, to] = dot3_turned(lefts, (v.high[to], v.low[to]))
-
-        @pl.when(block != row)
+        pl.when(ahead(block) == 0)(lambda: hand_beside(block).start())
+        pl.when(ahead(block) == 1)(lambda: away(block, 0, 1).start())
+        pl.when(ahead(block) == RING - 1)(lambda: away(block, 1, 0).start())
+
+        @pl.when(ahead(block) == 2)
         def _():
-            away(block, core).start()
-
-        @pl.when(block == row)
-        def _():
-            v.land[row, core] = v.prod[block, core]
-
-        away(block, 1 - core).start()
+            hop_to(block, 0).start()
+            hop_to(block, 1).start()
+
+    def add_and_pass(idx):
+        block = order(idx)
+        for side in range(2):
+
+            @pl.when(ahead(block) == (1, RING - 1)[side])
+            def _():
+                hop_to(block, side).wait_recv()
+                v.prod[block, side] = v.prod[block, side] + v.hop[block]
+                away(block, side, side).start()
+
+    def plane_sum(to_plane, part):
+        total = v.land[0, to_plane, part] + v.land[1, to_plane, part]
+        mine = jnp.where(core == part, 1, 0)
+        return total + jnp.where(mine == 1, v.prod[RING * to_plane + z, core], v.beside[to_plane])
+
+    def cross_to(part):
+        return copy(
+            v.cross.at[part],
+            v.cross_in.at[part],
+            v.cross_send.at[part],
+            v.cross_recv.at[part],
+            (RING * (1 - plane) + z, col),
+        )
+
+    def arrivals(to_plane):
+        copy(v.cross.at[0], v.beside.at[0], v.push.at[0, 0], v.beside_recv.at[to_plane], sibling).wait_recv()
+        for part in range(2):
+            for side in range(2):
+                copy(
+                    v.cross.at[0], v.cross_in.at[0], v.push.at[0, 0], v.landed.at[side, to_plane, part], sibling
+                ).wait_recv()
+
+    def cross():
+        arrivals(1 - plane)
+        for part in range(2):
+            v.cross[part] = plane_sum(1 - plane, part)
+            cross_to(part).start()
 
     def slice_to(other):
         return copy(
@@ -284,6 +351,7 @@
             copy(
                 v.slices.at[row], v.slices.at[source], v.cut.at[source], v.cut_in.at[source], (source, core)
             ).wait_recv()
+            slice_to(source).wait_send()
         total = v.slices[0]
         for other in range(1, n_rows):
             total = total + v.slices[other]
@@ -425,6 +493,7 @@
             copy(mine_ref, got.at[chip], v.send.at[0], v.recv.at[idx], at_right).wait_recv()
 
         product(idx)
+        pl.when(idx > 0)(lambda: add_and_pass(idx - 1))
 
         @pl.when(idx == 0)
         def _():
@@ -443,6 +512,7 @@
         return carry
 
     lax.fori_loop(0, CHIPS, body, 0)
+    add_and_pass(CHIPS - 1)
 
     lefts = split(got[chip])
     for side in range(2):
@@ -464,23 +534,15 @@
     give_total = copy(v.total.at[1 - core], v.total_in, v.total_send, v.total_recv, sibling)
     give_total.start()
 
-    for other in range(2):
-        for step in range(n_rows):
-            source = (row + step) % n_rows
-
-            @pl.when((step > 0) | (core != other))
-            def _():
-                copy(
-                    v.prod.at[0, 0], v.land.at[source, other], v.push.at[0, 0], v.landed.at[source, other], sibling
-                ).wait_recv()
-
-        total = v.land[0, other]
-        for source in range(1, n_rows):
-            total = total + v.land[source, other]
+    cross()
+    arrivals(plane)
+    for part in range(2):
+        cross_to(part).wait_recv()
+        total = plane_sum(plane, part) + v.cross_in[part]
         shape = (width, width)
-        shift = (row * 2 + other - (2 * chip + core)) * width
+        shift = (row * 2 + part - (2 * chip + core)) * width
         there = lax.broadcasted_iota(jnp.int32, shape, 0) + shift == lax.broadcasted_iota(jnp.int32, shape, 1)
-        gram_ref[pl.ds(other * width, width)] = jnp.where(there, 1.0, 0.0) + scale * total
+        gram_ref[pl.ds(part * width, width)] = jnp.where(there, 1.0, 0.0) + scale * total
 
     share = panel_ref.shape[0]
     other_span = pl.ds(pl.multiple_of((1 - core) * width, width), width)
@@ -513,7 +575,6 @@
     @pl.when(chip == 0)
     def _():
         for step in range(1, n_rows):
-            slice_to((row + step) % n_rows).wait_send()
             for to in range(2):
                 share_to(step, to).wait_send()
         share_to(0, 1 - core).wait_send()
@@ -528,10 +589,15 @@
     give_total.wait_send()
 
     def drain_push(block, carry):
-        pl.when(block != row)(lambda: away(block, core).wait_send())
-        away(block, 1 - core).wait_send()
+        pl.when(ahead(block) == 0)(lambda: hand_beside(block).wait_send())
+        for side in range(2):
+            pl.when(ahead(block) == 2)(lambda: hop_to(block, side).wait_send())
+            for to in range(2):
+                pl.when(ahead(block) == (1, RING - 1)[side])(lambda: away(block, side, to).wait_send())
         return carry
 
+    for part in range(2):
+        cross_to(part).wait_send()
     lax.fori_loop(0, CHIPS, drain_push, 0)
 
     def drain_chain(i, carry):

time: 190 us -> 147 us (0.77)
  the two profiles are of different devices: /device:TPU:47 before, /device:TPU:93 now
where the time goes in v5:
time: 147 us
  Pallas kernels  141 us (96%)
  local copies, waits for them, and re-layouts  5.4 us (4%)
    pallas_call x1, Pallas kernels, on_device(): pl.pallas_call(functools.partial(fused_kernel, tuple(scratch)), out_shape...  141 us
    unnamed x3, local copies, waits for them, and re-layouts  5.4 us

profile of v5, /device:TPU:93, one launch (start us, length us, event | category | flops | bytes accessed | tf_op | source)
XLA Modules:
  0.0 146.5 jit_solution(9589701325340327046)
XLA Ops:
  0.6 140.5 %shard_map.58 = (f32[512,256]{1,0:T(8,128)}, f32[32,512]{1,0:T(8,128)}, f32[768,256]{1,0:T(8,128)}) custom-call(f32[768,256]{1,0:T(8,128)} %mine_ref.1, f32[8,2,256,256]{3,2,1,0:T(8,128)} %bitcast.3, f32[8,2,256,512]{3,2,1,0:T(8,128)} %bitcast.2), custom_call_target="tpu_custom_call" | custom-call | flops 10000000000 | bytes 20000000 | tf_op jit(solution)/shard_map/pallas_call | solution.py:627
  141.1 1.9 %copy.9 = f32[512,256]{1,0:T(8,128)} copy(f32[512,256]{1,0:T(8,128)} %get-tuple-element.6) | data formatting | bytes 1048576
  143.0 1.5 %copy.10 = f32[32,512]{1,0:T(8,128)} copy(f32[32,512]{1,0:T(8,128)} %get-tuple-element.7) | data formatting | bytes 131072
  144.5 2.1 %copy.11 = f32[768,256]{1,0:T(8,128)} copy(f32[768,256]{1,0:T(8,128)} %get-tuple-element.8) | data formatting | bytes 1572864

commit v6 on v5

--- a/solution.py
+++ b/solution.py
@@ -36,9 +36,9 @@
     )
 
 
-def factor_block(grid):
+def factor_block(grid, first, last):
     base = grid.shape[0]
-    for p in range(base // 8):
+    for p in range(first, last):
         rows = slice(8 * p, 8 * p + 8)
         panel = grid[rows]
         sub = lax.broadcasted_iota(jnp.int32, panel.shape, 0)
@@ -64,20 +64,29 @@
             grid[rest] = value
 
 
-def factor_step(work, grid, inverted, below, s):
+def factor_part(work, grid, inverted, below, s, part):
     base = grid.shape[0]
     span = pl.ds(pl.multiple_of(s * base, base), base)
-    shape = (base, base)
-    eye = lax.broadcasted_iota(jnp.int32, shape, 0) == lax.broadcasted_iota(jnp.int32, shape, 1)
-    grid[:, :base] = work[span, span]
-    grid[:, base:] = jnp.where(eye, 1.0, 0.0)
-    factor_block(grid)
-    inverted[s] = grid[:, base:]
-    done = dot_exact_turned(work[:, span], grid[:, base:])
-    later = lax.broadcasted_iota(jnp.int32, done.shape, 0) >= (s + 1) * base
-    done = jnp.where(later, done, 0.0)
-    below[s] = done
-    work[...] = work[...] - dot_exact_turned(done, done)
+    panels = base // 8
+
+    @pl.when(part == 0)
+    def _():
+        shape = (base, base)
+        eye = lax.broadcasted_iota(jnp.int32, shape, 0) == lax.broadcasted_iota(jnp.int32, shape, 1)
+        grid[:, :base] = work[span, span]
+        grid[:, base:] = jnp.where(eye, 1.0, 0.0)
+        factor_block(grid, 0, panels * 2 // 5)
+
+    pl.when(part == 1)(lambda: factor_block(grid, panels * 2 // 5, panels))
+
+    @pl.when(part == 2)
+    def _():
+        inverted[s] = grid[:, base:]
+        done = dot_exact_turned(work[:, span], grid[:, base:])
+        later = lax.broadcasted_iota(jnp.int32, done.shape, 0) >= (s + 1) * base
+        done = jnp.where(later, done, 0.0)
+        below[s] = done
+        work[...] = work[...] - dot_exact_turned(done, done)
 
 
 def solve_rows(rows_ref, inverted, below):
@@ -130,8 +139,10 @@
         cols=vmem((CHIPS - 1, 2, width, width), f32),
         total=vmem((2, n, width), f32),
         total_in=vmem((n, width), f32),
-        send=dma((9,)),
-        recv=dma((9,)),
+        send=dma((13,)),
+        recv=dma((13,)),
+        theirs_send=dma,
+        theirs_recv=dma,
         push=dma((CHIPS, 2)),
         hop_send=dma((CHIPS, 2)),
         hop_recv=dma((CHIPS,)),
@@ -173,7 +184,6 @@
     x, y = chip % 4, chip // 4
     z, plane = row % RING, row // RING
     n, width = mine_ref.shape
-    half = n // 2
     piece = width // n_rows
     z_rows = width // RING
     scale = 3.0 / (n * n_rows)
@@ -198,21 +208,29 @@
         return 4 * ((y + dy) % 2) + (x + dx) % 4
 
     left, right, partner, far = at(3, 0), at(1, 0), at(0, 1), at(2, 0)
-    top, low_half = pl.ds(0, half), pl.ds(half, half)
     at_right, at_left = (row, 2 * right + core), (row, 2 * left + core)
     at_partner = (row, 2 * partner + core)
     got = v.got
-    sends = [
-        copy(mine_ref, v.theirs, v.send.at[8], v.recv.at[8], sibling),
-        copy(mine_ref, got.at[chip], v.send.at[0], v.recv.at[0], at_right),
-        copy(mine_ref, got.at[chip], v.send.at[1], v.recv.at[1], at_left),
-        copy(mine_ref, got.at[chip], v.send.at[2], v.recv.at[2], at_partner),
-        copy(got.at[left, top], got.at[left, top], v.send.at[3], v.recv.at[3], at_right),
-        copy(got.at[right, low_half], got.at[right, low_half], v.send.at[4], v.recv.at[4], at_left),
-        copy(got.at[partner], got.at[partner], v.send.at[5], v.recv.at[5], at_right),
-        copy(got.at[partner], got.at[partner], v.send.at[6], v.recv.at[6], at_left),
-        copy(got.at[far], got.at[far], v.send.at[7], v.recv.at[7], at_partner),
+    top, low_half = pl.ds(0, n // 2), pl.ds(n // 2, n // 2)
+
+    def block_copy(block, span, k, device, source=None):
+        place = got.at[block] if span is None else got.at[block, span]
+        return copy(place if source is None else source, place, v.send.at[k], v.recv.at[k], device)
+
+    own_sends = [
+        block_copy(chip, None, 0, at_right, mine_ref),
+        block_copy(chip, None, 1, at_left, mine_ref),
+        block_copy(chip, None, 2, at_partner, mine_ref),
     ]
+    half_sends = [block_copy(left, top, 3, at_right), block_copy(right, low_half, 4, at_left)]
+    thirds = [pl.ds(0, n * 3 // 8), pl.ds(n * 3 // 8, n * 3 // 8), pl.ds(n * 3 // 4, n // 4)]
+    partner_sends = [
+        [block_copy(partner, span, 5 + k, at_right), block_copy(partner, span, 8 + k, at_left)]
+        for k, span in enumerate(thirds)
+    ]
+    far_sends = [block_copy(far, top, 11, at_partner), block_copy(far, low_half, 12, at_partner)]
+
+    give_mine = copy(mine_ref, v.theirs, v.theirs_send, v.theirs_recv, sibling)
     give_factor = copy(factor_ref.at[:, 1 - core], v.their_factor, v.factor_send, v.factor_recv, sibling)
     own_span = pl.ds(pl.multiple_of(core * width, width), width)
     fetch = [
@@ -222,8 +240,10 @@
             inverses_ref.at[:, :, pl.ds(pl.multiple_of(z * z_rows, z_rows), z_rows), own_span], v.starts, v.local.at[2]
         ),
     ]
-    for one in sends[:4]:
-        one.start()
+    give_mine.start()
+    own_sends[0].start()
+    own_sends[1].start()
+    own_sends[2].start()
     give_factor.start()
     for one in fetch:
         one.start()
@@ -231,7 +251,7 @@
     own_high, own_low = split(mine_ref[...])
     v.high[core] = own_high
     v.low[core] = own_low
-    sends[0].wait_recv()
+    give_mine.wait_recv()
     their_high, their_low = split(v.theirs[...])
     v.high[1 - core] = their_high
     v.low[1 - core] = their_low
@@ -342,10 +362,12 @@
         rows = lead_rows(row, core)
         return copy(rows, rows, v.share.at[step, to], v.shared.at[row, core], ((row + step) % n_rows, to))
 
-    def lead_slices():
+    def lead_push():
         for step in range(1, n_rows):
             slice_to((row + step) % n_rows).start()
         v.slices[row] = v.prod[0, :, pl.ds(pl.multiple_of(row * piece, piece), piece)]
+
+    def lead_sum():
         for step in range(1, n_rows):
             source = (row + step) % n_rows
             copy(
@@ -459,7 +481,6 @@
         for one in spread(i):
             one.start()
         v.cols[i, core, z_span(z)] = v.own[i, core]
-        pl.when(i > 0)(lambda: couple(i - 1))
 
     def relay(i):
         for side in range(2):
@@ -474,67 +495,118 @@
         v.inverse_high[side] = high
         v.inverse_low[side] = low
 
-    def body(idx, carry):
-        @pl.when(idx == 1)
+    def accumulate(idx):
+        i = order(idx)
+
+        @pl.when(i < chip)
         def _():
-            for one in sends[1:4]:
-                one.wait_recv()
-            for one in sends[4:8]:
-                one.start()
-
-        @pl.when(idx == 4)
-        def _():
-            sends[4].wait_recv()
-            sends[5].wait_recv()
-            sends[8].start()
-
-        @pl.when(idx > 4)
-        def _():
-            copy(mine_ref, got.at[chip], v.send.at[0], v.recv.at[idx], at_right).wait_recv()
-
-        product(idx)
-        pl.when(idx > 0)(lambda: add_and_pass(idx - 1))
-
-        @pl.when(idx == 0)
-        def _():
-            pl.when(chip == 0)(lead_slices)
-            give_factor.wait_recv()
-            pl.when(chip > 0)(lambda: couple(chip - 1))
-
-        pl.when((idx < CHIPS - 1) & (chip > idx))(lambda: chain_step(idx + 1))
-        pl.when((idx > 0) & (chip >= idx))(lambda: relay(chip - idx))
-
-        @pl.when((idx >= 4) & (chip == 0))
-        def _():
-            pl.when(idx == 4)(lead_wait)
-            factor_step(v.work, v.grid, v.inverted, v.below, idx - 4)
-
+            arrived(i, 1 - core, 0).wait_recv()
+            for side in range(2):
+                for slot in (3, 4):
+                    arrived(i, side, slot).wait_recv()
+            lefts = split(got[i])
+            for side in range(2):
+                v.total[side] = v.total[side] + dot3(lefts, split(v.cols[i, side]))
+
+    product(0)
+    pl.when(chip == 0)(lead_push)
+    give_factor.wait_recv()
+
+    def couple_one(j, carry):
+        couple(j)
         return carry
 
-    lax.fori_loop(0, CHIPS, body, 0)
-    add_and_pass(CHIPS - 1)
-
+    lax.fori_loop(0, chip, couple_one, 0)
     lefts = split(got[chip])
     for side in range(2):
         span = slice(side * width, (side + 1) * width)
         v.total[side] = dot3(lefts, (v.inverse_high[core, :, span], v.inverse_low[core, :, span]))
 
-    def accumulate(step, carry):
-        i = chip - 1 - step
-        arrived(i, 1 - core, 0).wait_recv()
-        for side in range(2):
-            for slot in (3, 4):
-                arrived(i, side, slot).wait_recv()
-        lefts = split(got[i])
-        for side in range(2):
-            v.total[side] = v.total[side] + dot3(lefts, split(v.cols[i, side]))
+    def one_solved(idx, carry):
+        accumulate(idx)
         return carry
 
-    lax.fori_loop(0, chip, accumulate, 0)
+    def by_stage(stage, table):
+        first, last = 0, 0
+        for key, (low, high) in table.items():
+            first = jnp.where(stage == key, low, first)
+            last = jnp.where(stage == key, high, last)
+        return first, last
+
+    def body(stage, carry):
+        @pl.when(stage == 1)
+        def _():
+            for one in own_sends[:2]:
+                one.wait_recv()
+            for one in half_sends:
+                one.start()
+
+        @pl.when(stage == 2)
+        def _():
+            for one in half_sends:
+                one.wait_recv()
+            for one in far_sends:
+                one.start()
+
+        pl.when(chip > stage)(lambda: chain_step(stage + 1))
+
+        @pl.when(stage == 1)
+        def _():
+            own_sends[2].wait_recv()
+
+        for k in range(3):
+
+            @pl.when(stage == k + 1)
+            def _():
+                for one in partner_sends[k]:
+                    one.start()
+
+        @pl.when(stage == 4)
+        def _():
+            for one in sum(partner_sends, far_sends):
+                one.wait_recv()
+
+        def one_product(idx, carry):
+            product(idx)
+            return carry
+
+        def one_pass(idx, carry):
+            add_and_pass(idx)
+            return carry
+
+        def one_part(step, carry):
+            pl.when(step == 0)(lead_wait)
+            factor_part(v.work, v.grid, v.inverted, v.below, step // 3, step % 3)
+            return carry
+
+        lax.fori_loop(*by_stage(stage, {1: (1, 4), 2: (4, 5), 4: (5, 8)}), one_product, 0)
+        pl.when((stage > 0) & (chip >= stage))(lambda: relay(chip - stage))
+        lax.fori_loop(*by_stage(stage, {2: (0, 4), 3: (4, 5), 5: (5, 8)}), one_pass, 0)
+
+        @pl.when(chip == 0)
+        def _():
+            pl.when(stage == 1)(lead_sum)
+            lax.fori_loop(*by_stage(stage, {2: (0, 3), 3: (3, 6), 4: (6, 9), 5: (9, 12)}), one_part, 0)
+
+        lax.fori_loop(*by_stage(stage, {5: (1, 3), 6: (3, 5)}), one_solved, 0)
+
+        return carry
+
+    lax.fori_loop(0, CHIPS - 1, body, 0)
+    pl.when(chip == CHIPS - 1)(lambda: relay(0))
+    cross()
+
+    lax.fori_loop(5, CHIPS, one_solved, 0)
     give_total = copy(v.total.at[1 - core], v.total_in, v.total_send, v.total_recv, sibling)
     give_total.start()
 
-    cross()
+    @pl.when(chip == 0)
+    def _():
+        shape = (2 * width, 2 * width)
+        eye = lax.broadcasted_iota(jnp.int32, shape, 0) == lax.broadcasted_iota(jnp.int32, shape, 1)
+        v.work[...] = jnp.where(eye, 1.0, 0.0)
+        solve_rows(v.work, v.inverted, v.below)
+
     arrivals(plane)
     for part in range(2):
         cross_to(part).wait_recv()
@@ -559,7 +631,9 @@
         v.first[:, own_span] = gram_ref[own_span]
         swap.wait_recv()
         v.first[:, other_span] = v.side[...]
-        solve_rows(v.first, v.inverted, v.below)
+        v.first[...] = jnp.dot(
+            v.first[...], v.work[...], precision=lax.Precision.HIGHEST, preferred_element_type=jnp.float32
+        )
         for m in range(1, CHIPS):
             hand_out(m).start()
         pl.when(core == 1)(lambda: hand_out(0).start())
@@ -583,8 +657,9 @@
             hand_out(m).wait_send()
         pl.when(core == 1)(lambda: hand_out(0).wait_send())
 
-    for one in sends:
+    for one in sum(partner_sends, own_sends + half_sends + far_sends):
         one.wait_send()
+    give_mine.wait_send()
     give_factor.wait_send()
     give_total.wait_send()
 
@@ -618,13 +693,28 @@
     lax.fori_loop(0, chip, drain_chain, 0)
 
 
+def finish_kernel(*refs):
+    for source, target in zip(refs[:3], refs[3:]):
+        target[...] = source[...]
+
+
+def finish(values):
+    vmem = pl.BlockSpec(memory_space=pltpu.VMEM)
+    return pl.pallas_call(
+        finish_kernel,
+        out_shape=tuple(jax.ShapeDtypeStruct(a.shape, a.dtype) for a in values),
+        in_specs=[vmem] * 3,
+        out_specs=(vmem,) * 3,
+    )(*values)
+
+
 def on_device(iterate, factor, inverses):
     n, width = iterate.shape
     n_rows = lax.axis_size("row")
     n_cols = lax.axis_size("col")
     vmem = pl.BlockSpec(memory_space=pltpu.VMEM)
     scratch = scratch_shapes(n, width, n_rows)
-    return pl.pallas_call(
+    values = pl.pallas_call(
         functools.partial(fused_kernel, tuple(scratch)),
         out_shape=(
             jax.ShapeDtypeStruct((2 * width, width), jnp.float32),
@@ -639,6 +729,7 @@
         ),
         cost_estimate=pl.CostEstimate(flops=10**10, bytes_accessed=2 * 10**7, transcendentals=0),
     )(iterate, factor.reshape(CHIPS, 2, width, width), inverses.reshape(CHIPS, 2, width, 2 * width))
+    return finish(values)
 
 
 def solution(mesh):

time: 147 us -> 133 us (0.905)
  the two profiles are of different devices: /device:TPU:93 before, /device:TPU:1 now
where the time goes in v6:
time: 133 us
  Pallas kernels  133 us (100%)
    pallas_call x1, Pallas kernels, on_device(): pl.pallas_call(functools.partial(fused_kernel, tuple(scratch)), out_shape...  130 us

profile of v6, /device:TPU:1, one launch (start us, length us, event | category | flops | bytes accessed | tf_op | source)
XLA Modules:
  0.0 133.2 jit_solution(93185745482246552)
XLA Ops:
  0.6 130.1 %shard_map.58 = (f32[512,256]{1,0:T(8,128)}, f32[32,512]{1,0:T(8,128)}, f32[768,256]{1,0:T(8,128)}) custom-call(f32[768,256]{1,0:T(8,128)} %mine_ref.1, f32[8,2,256,256]{3,2,1,0:T(8,128)} %bitcast.3, f32[8,2,256,512]{3,2,1,0:T(8,128)} %bitcast.2), custom_call_target="tpu_custom_call" | custom-call | flops 10000000000 | bytes 20000000 | tf_op jit(solution)/shard_map/pallas_call | solution.py:717
  130.8 2.4 %shard_map.59 = (f32[512,256]{1,0:T(8,128)}, f32[32,512]{1,0:T(8,128)}, f32[768,256]{1,0:T(8,128)}) custom-call(f32[512,256]{1,0:T(8,128)} %get-tuple-element.6.refs_0_, f32[32,512]{1,0:T(8,128)} %get-tuple-element.7.refs_1_, f32[768,256]{1,0:T(8,128)} %get-tuple-element.8.refs_2_), custom_call_target="tpu_custom_call" | custom-call | tf_op jit(solution)/shard_map/pallas_call | solution.py:703

commit v7 on v6

--- a/solution.py
+++ b/solution.py
@@ -43,17 +43,15 @@
         panel = grid[rows]
         sub = lax.broadcasted_iota(jnp.int32, panel.shape, 0)
         columns = [jnp.broadcast_to(panel[:, 8 * p + c : 8 * p + c + 1], panel.shape) for c in range(8)]
-        scales = jnp.zeros_like(panel)
+        scales = jnp.ones_like(panel)
         for j in range(8):
             pivot = jnp.broadcast_to(columns[j][j : j + 1], panel.shape)
-            guess = lax.rsqrt(pivot)
-            guess = guess * (1.5 - 0.5 * pivot * guess * guess)
-            below = jnp.where(sub > j, columns[j] * (guess * guess), 0.0)
-            scales = jnp.where(sub == j, guess, scales)
+            below = jnp.where(sub > j, columns[j], 0.0) / pivot
+            scales = jnp.where(sub == j, pivot, scales)
             for c in range(j + 1, 8):
                 columns[c] = columns[c] - below * columns[c][j : j + 1]
             panel = panel - below * panel[j : j + 1]
-        panel = panel * scales
+        panel = panel / jnp.sqrt(scales)
         grid[rows] = panel
         if 8 * p + 8 < base:
             rest = slice(8 * p + 8, base)
@@ -82,11 +80,18 @@
     @pl.when(part == 2)
     def _():
         inverted[s] = grid[:, base:]
-        done = dot_exact_turned(work[:, span], grid[:, base:])
-        later = lax.broadcasted_iota(jnp.int32, done.shape, 0) >= (s + 1) * base
-        done = jnp.where(later, done, 0.0)
-        below[s] = done
-        work[...] = work[...] - dot_exact_turned(done, done)
+
+        @pl.when((s + 1) * base == work.shape[0])
+        def _():
+            below[s] = jnp.zeros(below.shape[1:], jnp.float32)
+
+        @pl.when((s + 1) * base < work.shape[0])
+        def _():
+            done = dot_exact_turned(work[:, span], grid[:, base:])
+            later = lax.broadcasted_iota(jnp.int32, done.shape, 0) >= (s + 1) * base
+            done = jnp.where(later, done, 0.0)
+            below[s] = done
+            work[...] = work[...] - dot_exact_turned(done, done)
 
 
 def solve_rows(rows_ref, inverted, below):
@@ -143,13 +148,13 @@
         recv=dma((13,)),
         theirs_send=dma,
         theirs_recv=dma,
-        push=dma((CHIPS, 2)),
-        hop_send=dma((CHIPS, 2)),
-        hop_recv=dma((CHIPS,)),
-        landed=dma((2, 2, 2)),
+        push=dma((CHIPS, 2, 2)),
+        hop_send=dma((CHIPS, 2, 2)),
+        hop_recv=dma((CHIPS, 2)),
+        landed=dma((2, 2, 2, 2)),
         beside_recv=dma((2,)),
-        cross_send=dma((2,)),
-        cross_recv=dma((2,)),
+        cross_send=dma((2, 2)),
+        cross_recv=dma((2, 2)),
         cut=dma((n_rows,)),
         cut_in=dma((n_rows,)),
         share=dma((n_rows, 2)),
@@ -269,19 +274,25 @@
     def z_peer(step, to):
         return (RING * plane + (z + step) % RING, 2 * chip + to)
 
-    def hop_to(block, side):
+    halves = [pl.ds(0, width // 2), pl.ds(width // 2, width // 2)]
+
+    def hop_to(block, side, c):
         step = (1, RING - 1)[side]
         return copy(
-            v.prod.at[block, side], v.hop.at[block], v.hop_send.at[block, side], v.hop_recv.at[block], z_peer(step, core)
-        )
-
-    def away(block, side, to):
+            v.prod.at[block, side, halves[c]],
+            v.hop.at[block, halves[c]],
+            v.hop_send.at[block, side, c],
+            v.hop_recv.at[block, c],
+            z_peer(step, core),
+        )
+
+    def away(block, side, to, c):
         step = (1, RING - 1)[side]
         return copy(
-            v.prod.at[block, to],
-            v.land.at[side, block // RING, core],
-            v.push.at[block, to],
-            v.landed.at[side, block // RING, core],
+            v.prod.at[block, to, halves[c]],
+            v.land.at[side, block // RING, core, halves[c]],
+            v.push.at[block, to, c],
+            v.landed.at[side, block // RING, core, c],
             z_peer(step, to),
         )
 
@@ -289,7 +300,7 @@
         return copy(
             v.prod.at[block, 1 - core],
             v.beside.at[block // RING],
-            v.push.at[block, 1 - core],
+            v.push.at[block, 1 - core, 0],
             v.beside_recv.at[block // RING],
             sibling,
         )
@@ -300,13 +311,19 @@
         for to in range(2):
             v.prod[block, to] = dot3_turned(lefts, (v.high[to], v.low[to]))
         pl.when(ahead(block) == 0)(lambda: hand_beside(block).start())
-        pl.when(ahead(block) == 1)(lambda: away(block, 0, 1).start())
-        pl.when(ahead(block) == RING - 1)(lambda: away(block, 1, 0).start())
 
         @pl.when(ahead(block) == 2)
         def _():
-            hop_to(block, 0).start()
-            hop_to(block, 1).start()
+            for c in range(2):
+                for side in range(2):
+                    hop_to(block, side, c).start()
+
+        for side in range(2):
+
+            @pl.when(ahead(block) == (1, RING - 1)[side])
+            def _():
+                for c in range(2):
+                    away(block, side, 1 - side, c).start()
 
     def add_and_pass(idx):
         block = order(idx)
@@ -314,37 +331,46 @@
 
             @pl.when(ahead(block) == (1, RING - 1)[side])
             def _():
-                hop_to(block, side).wait_recv()
-                v.prod[block, side] = v.prod[block, side] + v.hop[block]
-                away(block, side, side).start()
-
-    def plane_sum(to_plane, part):
-        total = v.land[0, to_plane, part] + v.land[1, to_plane, part]
+                for c in range(2):
+                    rows = halves[c]
+                    hop_to(block, side, c).wait_recv()
+                    v.prod[block, side, rows] = v.prod[block, side, rows] + v.hop[block, rows]
+                    away(block, side, side, c).start()
+
+    def plane_sum(to_plane, part, c):
+        rows = halves[c]
+        total = v.land[0, to_plane, part, rows] + v.land[1, to_plane, part, rows]
         mine = jnp.where(core == part, 1, 0)
-        return total + jnp.where(mine == 1, v.prod[RING * to_plane + z, core], v.beside[to_plane])
-
-    def cross_to(part):
+        return total + jnp.where(mine == 1, v.prod[RING * to_plane + z, core, rows], v.beside[to_plane, rows])
+
+    def cross_to(part, c):
         return copy(
-            v.cross.at[part],
-            v.cross_in.at[part],
-            v.cross_send.at[part],
-            v.cross_recv.at[part],
+            v.cross.at[part, halves[c]],
+            v.cross_in.at[part, halves[c]],
+            v.cross_send.at[part, c],
+            v.cross_recv.at[part, c],
             (RING * (1 - plane) + z, col),
         )
 
-    def arrivals(to_plane):
-        copy(v.cross.at[0], v.beside.at[0], v.push.at[0, 0], v.beside_recv.at[to_plane], sibling).wait_recv()
+    def arrivals(to_plane, c):
+        if c == 0:
+            copy(v.cross.at[0], v.beside.at[0], v.push.at[0, 0, 0], v.beside_recv.at[to_plane], sibling).wait_recv()
         for part in range(2):
             for side in range(2):
                 copy(
-                    v.cross.at[0], v.cross_in.at[0], v.push.at[0, 0], v.landed.at[side, to_plane, part], sibling
+                    v.cross.at[0, halves[0]],
+                    v.cross_in.at[0, halves[0]],
+                    v.push.at[0, 0, 0],
+                    v.landed.at[side, to_plane, part, c],
+                    sibling,
                 ).wait_recv()
 
     def cross():
-        arrivals(1 - plane)
-        for part in range(2):
-            v.cross[part] = plane_sum(1 - plane, part)
-            cross_to(part).start()
+        for c in range(2):
+            arrivals(1 - plane, c)
+            for part in range(2):
+                v.cross[part, halves[c]] = plane_sum(1 - plane, part, c)
+                cross_to(part, c).start()
 
     def slice_to(other):
         return copy(
@@ -586,7 +612,7 @@
         @pl.when(chip == 0)
         def _():
             pl.when(stage == 1)(lead_sum)
-            lax.fori_loop(*by_stage(stage, {2: (0, 3), 3: (3, 6), 4: (6, 9), 5: (9, 12)}), one_part, 0)
+            lax.fori_loop(*by_stage(stage, {2: (0, 2), 3: (2, 5), 4: (5, 9), 5: (9, 12)}), one_part, 0)
 
         lax.fori_loop(*by_stage(stage, {5: (1, 3), 6: (3, 5)}), one_solved, 0)
 
@@ -607,14 +633,17 @@
         v.work[...] = jnp.where(eye, 1.0, 0.0)
         solve_rows(v.work, v.inverted, v.below)
 
-    arrivals(plane)
-    for part in range(2):
-        cross_to(part).wait_recv()
-        total = plane_sum(plane, part) + v.cross_in[part]
-        shape = (width, width)
-        shift = (row * 2 + part - (2 * chip + core)) * width
-        there = lax.broadcasted_iota(jnp.int32, shape, 0) + shift == lax.broadcasted_iota(jnp.int32, shape, 1)
-        gram_ref[pl.ds(part * width, width)] = jnp.where(there, 1.0, 0.0) + scale * total
+    for c in range(2):
+        arrivals(plane, c)
+        for part in range(2):
+            cross_to(part, c).wait_recv()
+            total = plane_sum(plane, part, c) + v.cross_in[part, halves[c]]
+            shift = (row * 2 + part - (2 * chip + core)) * width + c * (width // 2)
+            there = lax.broadcasted_iota(jnp.int32, total.shape, 0) + shift == lax.broadcasted_iota(
+                jnp.int32, total.shape, 1
+            )
+            rows = pl.ds(part * width + c * (width // 2), width // 2)
+            gram_ref[rows] = jnp.where(there, 1.0, 0.0) + scale * total
 
     share = panel_ref.shape[0]
     other_span = pl.ds(pl.multiple_of((1 - core) * width, width), width)
@@ -665,14 +694,16 @@
 
     def drain_push(block, carry):
         pl.when(ahead(block) == 0)(lambda: hand_beside(block).wait_send())
-        for side in range(2):
-            pl.when(ahead(block) == 2)(lambda: hop_to(block, side).wait_send())
-            for to in range(2):
-                pl.when(ahead(block) == (1, RING - 1)[side])(lambda: away(block, side, to).wait_send())
+        for c in range(2):
+            for side in range(2):
+                pl.when(ahead(block) == 2)(lambda: hop_to(block, side, c).wait_send())
+                for to in range(2):
+                    pl.when(ahead(block) == (1, RING - 1)[side])(lambda: away(block, side, to, c).wait_send())
         return carry
 
     for part in range(2):
-        cross_to(part).wait_send()
+        for c in range(2):
+            cross_to(part, c).wait_send()
     lax.fori_loop(0, CHIPS, drain_push, 0)
 
     def drain_chain(i, carry):

time: 133 us -> 130 us (0.977)
  the two profiles are of different devices: /device:TPU:1 before, /device:TPU:14 now
where the time goes in v7:
time: 130 us
  Pallas kernels  129 us (99%)
    pallas_call x1, Pallas kernels, on_device(): pl.pallas_call(functools.partial(fused_kernel, tuple(scratch)), out_shape...  127 us

profile of v7, /device:TPU:14, one launch (start us, length us, event | category | flops | bytes accessed | tf_op | source)
XLA Modules:
  0.0 129.6 jit_solution(15684075044576268301)
XLA Ops:
  0.6 126.6 %shard_map.58 = (f32[512,256]{1,0:T(8,128)}, f32[32,512]{1,0:T(8,128)}, f32[768,256]{1,0:T(8,128)}) custom-call(f32[768,256]{1,0:T(8,128)} %mine_ref.1, f32[8,2,256,256]{3,2,1,0:T(8,128)} %bitcast.3, f32[8,2,256,512]{3,2,1,0:T(8,128)} %bitcast.2), custom_call_target="tpu_custom_call" | custom-call | flops 10000000000 | bytes 20000000 | tf_op jit(solution)/shard_map/pallas_call | solution.py:748
  127.2 2.4 %shard_map.59 = (f32[512,256]{1,0:T(8,128)}, f32[32,512]{1,0:T(8,128)}, f32[768,256]{1,0:T(8,128)}) custom-call(f32[512,256]{1,0:T(8,128)} %get-tuple-element.6.refs_0_, f32[32,512]{1,0:T(8,128)} %get-tuple-element.7.refs_1_, f32[768,256]{1,0:T(8,128)} %get-tuple-element.8.refs_2_), custom_call_target="tpu_custom_call" | custom-call | tf_op jit(solution)/shard_map/pallas_call | solution.py:734

commit v8 on v7

--- a/solution.py
+++ b/solution.py
@@ -134,13 +134,13 @@
         inverse=vmem((2, width, 2 * width), f32),
         inverse_high=vmem((2, width, 2 * width), bf16),
         inverse_low=vmem((2, width, 2 * width), bf16),
-        starts=vmem((CHIPS, 2, z_rows, width), f32),
+        starts=vmem((CHIPS, z_rows, width), f32),
         w_high=vmem((CHIPS - 1, width, 2 * width), bf16),
         w_low=vmem((CHIPS - 1, width, 2 * width), bf16),
-        chain=vmem((CHIPS - 1, CHIPS - 1, 2, z_rows, width), f32),
-        part=vmem((CHIPS, 2, 2, z_rows, width), f32),
-        part_in=vmem((CHIPS, 2, z_rows, width), f32),
-        own=vmem((CHIPS - 1, 2, z_rows, width), f32),
+        chain=vmem((CHIPS - 1, CHIPS - 1, z_rows, width), f32),
+        part=vmem((CHIPS, 2, z_rows, width), f32),
+        part_in=vmem((CHIPS, z_rows, width), f32),
+        own=vmem((CHIPS - 1, z_rows, width), f32),
         cols=vmem((CHIPS - 1, 2, width, width), f32),
         total=vmem((2, n, width), f32),
         total_in=vmem((n, width), f32),
@@ -166,7 +166,9 @@
         part_recv=dma((CHIPS,)),
         chain_send=dma((CHIPS, CHIPS)),
         chain_recv=dma((CHIPS, CHIPS)),
-        col_send=dma((CHIPS, 5)),
+        seed_send=dma((CHIPS, 2)),
+        seed_recv=dma((CHIPS, 2)),
+        near_send=dma((CHIPS, 2, 2)),
         col_relay=dma((CHIPS, 2, 2)),
         col_recv=dma((CHIPS, 5, 2)),
         total_send=dma,
@@ -242,7 +244,7 @@
         pltpu.make_async_copy(inverses_ref.at[chip, 0], v.inverse.at[0], v.local.at[0]),
         pltpu.make_async_copy(inverses_ref.at[chip, 1], v.inverse.at[1], v.local.at[1]),
         pltpu.make_async_copy(
-            inverses_ref.at[:, :, pl.ds(pl.multiple_of(z * z_rows, z_rows), z_rows), own_span], v.starts, v.local.at[2]
+            inverses_ref.at[:, plane, pl.ds(pl.multiple_of(z * z_rows, z_rows), z_rows), own_span], v.starts, v.local.at[2]
         ),
     ]
     give_mine.start()
@@ -446,21 +448,40 @@
     def z_device(step, to):
         return (RING * plane + (z + step) % RING, 2 * chip + to)
 
-    def spread(i):
+    def seed_beside(i):
         place = v.cols.at[i, core, z_span(z)]
-        copies = [copy(v.own.at[i, 1 - core], place, v.col_send.at[i, 0], v.col_recv.at[i, 0, core], sibling)]
-        for slot, step in ((1, 1), (2, RING - 1)):
-            for to in range(2):
-                copies.append(
-                    copy(
-                        v.own.at[i, to],
-                        place,
-                        v.col_send.at[i, 2 * slot - 1 + to],
-                        v.col_recv.at[i, slot, core],
-                        z_device(step, to),
-                    )
-                )
-        return copies
+        return copy(v.own.at[i], place, v.seed_send.at[i, 0], v.seed_recv.at[i, core], sibling)
+
+    def seed_across(i):
+        place = v.cols.at[i, core, z_span(z)]
+        device = (RING * (1 - plane) + z, 2 * chip + plane)
+        return copy(v.own.at[i], place, v.seed_send.at[i, 1], v.seed_recv.at[i, core], device)
+
+    def near(i, side, slot):
+        place = v.cols.at[i, side, z_span(z)]
+        step = (1, RING - 1)[slot - 1]
+        return copy(
+            place, place, v.near_send.at[i, side, slot - 1], v.col_recv.at[i, slot, side], z_device(step, core)
+        )
+
+    def plant(i):
+        seed_across(i).start()
+        pl.when(core != plane)(lambda: seed_beside(i).start())
+
+        @pl.when(core == plane)
+        def _():
+            v.cols[i, core, z_span(z)] = v.own[i]
+
+    def relay_near(i):
+        for side in range(2):
+
+            @pl.when((core != plane) | (core != side))
+            def _():
+                place = v.cols.at[i, side, z_span(z)]
+                copy(place, place, v.seed_send.at[i, 0], v.seed_recv.at[i, side], sibling).wait_recv()
+
+            for slot in (1, 2):
+                near(i, side, slot).start()
 
     def onward(i, side, slot):
         step, start = ((1, 0), (RING - 1, z_rows // 2))[slot - 1]
@@ -472,22 +493,21 @@
     def arrived(i, side, slot):
         rows = z_span(z) if slot < 3 else z_span(z, 0, z_rows // 2)
         place = v.cols.at[i, side, rows]
-        return copy(place, place, v.col_send.at[i, 0], v.col_recv.at[i, slot, side], sibling)
+        return copy(place, place, v.seed_send.at[i, 0], v.col_recv.at[i, slot, side], sibling)
 
     def chain_step(d):
         i = chip - d
 
         def term(left, j):
-            left = left.reshape(2 * z_rows, width)
-            return dot3(split(left), (v.w_high[j], v.w_low[j])).reshape(2, z_rows, 2 * width)
+            return dot3(split(left), (v.w_high[j], v.w_low[j]))
 
         def add(value):
             for side in range(2):
-                v.part[d, side] = v.part[d, side] + value[:, :, side * width : (side + 1) * width]
+                v.part[d, side] = v.part[d, side] + value[:, side * width : (side + 1) * width]
 
         value = term(v.starts[i], i)
         for side in range(2):
-            v.part[d, side] = value[:, :, side * width : (side + 1) * width]
+            v.part[d, side] = value[:, side * width : (side + 1) * width]
 
         def more(j, carry):
             copy(v.own.at[i], v.chain.at[i, j], v.chain_send.at[i, 0], v.chain_recv.at[i, j], sibling).wait_recv()
@@ -504,11 +524,9 @@
             return carry
 
         lax.fori_loop(chip + 1, CHIPS, tell, 0)
-        for one in spread(i):
-            one.start()
-        v.cols[i, core, z_span(z)] = v.own[i, core]
-
-    def relay(i):
+        plant(i)
+
+    def relay_far(i):
         for side in range(2):
             for slot in (1, 2):
                 arrived(i, side, slot).wait_recv()
@@ -526,7 +544,6 @@
 
         @pl.when(i < chip)
         def _():
-            arrived(i, 1 - core, 0).wait_recv()
             for side in range(2):
                 for slot in (3, 4):
                     arrived(i, side, slot).wait_recv()
@@ -606,7 +623,8 @@
             return carry
 
         lax.fori_loop(*by_stage(stage, {1: (1, 4), 2: (4, 5), 4: (5, 8)}), one_product, 0)
-        pl.when((stage > 0) & (chip >= stage))(lambda: relay(chip - stage))
+        pl.when((stage > 0) & (chip >= stage))(lambda: relay_near(chip - stage))
+        pl.when((stage > 1) & (chip >= stage - 1))(lambda: relay_far(chip - stage + 1))
         lax.fori_loop(*by_stage(stage, {2: (0, 4), 3: (4, 5), 5: (5, 8)}), one_pass, 0)
 
         @pl.when(chip == 0)
@@ -619,7 +637,9 @@
         return carry
 
     lax.fori_loop(0, CHIPS - 1, body, 0)
-    pl.when(chip == CHIPS - 1)(lambda: relay(0))
+    pl.when(chip == CHIPS - 1)(lambda: relay_near(0))
+    pl.when(chip >= CHIPS - 2)(lambda: relay_far(chip - CHIPS + 2))
+    pl.when(chip == CHIPS - 1)(lambda: relay_far(0))
     cross()
 
     lax.fori_loop(5, CHIPS, one_solved, 0)
@@ -714,10 +734,11 @@
             return carry
 
         lax.fori_loop(chip + 1, CHIPS, told, 0)
-        for one in spread(i):
-            one.wait_send()
+        seed_across(i).wait_send()
+        pl.when(core != plane)(lambda: seed_beside(i).wait_send())
         for side in range(2):
             for slot in (1, 2):
+                near(i, side, slot).wait_send()
                 onward(i, side, slot).wait_send()
         return carry
 

time: 130 us -> 124 us (0.954)
  Pallas kernels: 129 us -> 123 us
    pallas_call x1, Pallas kernels: 127 us -> 120 us  [on_device(): pl.pallas_call(functools.partial(fused_kernel, tuple(scratch)), out_shape...]
where the time goes in v8:
time: 124 us; the launch traced here: 123 us
  Pallas kernels  123 us (99%)
    pallas_call x1, Pallas kernels, on_device(): pl.pallas_call(functools.partial(fused_kernel, tuple(scratch)), out_shape...  120 us

profile of v8, /device:TPU:14, one launch (start us, length us, event | category | flops | bytes accessed | tf_op | source)
XLA Modules:
  0.0 123.4 jit_solution(17001897987741561414)
XLA Ops:
  0.6 120.4 %shard_map.58 = (f32[512,256]{1,0:T(8,128)}, f32[32,512]{1,0:T(8,128)}, f32[768,256]{1,0:T(8,128)}) custom-call(f32[768,256]{1,0:T(8,128)} %mine_ref.1, f32[8,2,256,256]{3,2,1,0:T(8,128)} %bitcast.3, f32[8,2,256,512]{3,2,1,0:T(8,128)} %bitcast.2), custom_call_target="tpu_custom_call" | custom-call | flops 10000000000 | bytes 20000000 | tf_op jit(solution)/shard_map/pallas_call | solution.py:769
  121.0 2.4 %shard_map.59 = (f32[512,256]{1,0:T(8,128)}, f32[32,512]{1,0:T(8,128)}, f32[768,256]{1,0:T(8,128)}) custom-call(f32[512,256]{1,0:T(8,128)} %get-tuple-element.6.refs_0_, f32[32,512]{1,0:T(8,128)} %get-tuple-element.7.refs_1_, f32[768,256]{1,0:T(8,128)} %get-tuple-element.8.refs_2_), custom_call_target="tpu_custom_call" | custom-call | tf_op jit(solution)/shard_map/pallas_call | solution.py:755

commit v9 on v8

--- a/solution.py
+++ b/solution.py
@@ -130,6 +130,7 @@
         lead_in=vmem((2 * width, 2 * width), f32),
         first=vmem((width, 2 * width), f32),
         side=vmem((width, width), f32),
+        my_factor=vmem((CHIPS, width, width), f32),
         their_factor=vmem((CHIPS, width, width), f32),
         inverse=vmem((2, width, 2 * width), f32),
         inverse_high=vmem((2, width, 2 * width), bf16),
@@ -159,7 +160,7 @@
         cut_in=dma((n_rows,)),
         share=dma((n_rows, 2)),
         shared=dma((n_rows, 2)),
-        local=dma((3,)),
+        local=dma((4,)),
         factor_send=dma,
         factor_recv=dma,
         part_send=dma((CHIPS,)),
@@ -241,6 +242,7 @@
     give_factor = copy(factor_ref.at[:, 1 - core], v.their_factor, v.factor_send, v.factor_recv, sibling)
     own_span = pl.ds(pl.multiple_of(core * width, width), width)
     fetch = [
+        pltpu.make_async_copy(factor_ref.at[:, core], v.my_factor, v.local.at[3]),
         pltpu.make_async_copy(inverses_ref.at[chip, 0], v.inverse.at[0], v.local.at[0]),
         pltpu.make_async_copy(inverses_ref.at[chip, 1], v.inverse.at[1], v.local.at[1]),
         pltpu.make_async_copy(
@@ -429,7 +431,7 @@
 
     def couple(j):
         pairs = [(v.inverse_high[side], v.inverse_low[side]) for side in (core, 1 - core)]
-        value = dot3(split(factor_ref[j, core]), pairs[0]) + dot3(split(v.their_factor[j]), pairs[1])
+        value = dot3(split(v.my_factor[j]), pairs[0]) + dot3(split(v.their_factor[j]), pairs[1])
         w_high, w_low = split(value)
         v.w_high[j] = w_high
         v.w_low[j] = w_low
@@ -773,7 +775,7 @@
             jax.ShapeDtypeStruct((2 * width // n_cols, 2 * width), jnp.float32),
             jax.ShapeDtypeStruct((n, width), jnp.float32),
         ),
-        in_specs=[vmem, vmem, pl.BlockSpec(memory_space=pl.ANY)],
+        in_specs=[vmem, pl.BlockSpec(memory_space=pl.ANY), pl.BlockSpec(memory_space=pl.ANY)],
         out_specs=(vmem, vmem, vmem),
         scratch_shapes=list(scratch.values()),
         compiler_params=pltpu.CompilerParams(

time: 124 us -> 122 us (0.984)
    pallas_call x1, Pallas kernels: 120 us -> 119 us  [on_device(): pl.pallas_call(functools.partial(fused_kernel, tuple(scratch)), out_shape...]
where the time goes in v9:
time: 122 us
  Pallas kernels  122 us (100%)
    pallas_call x1, Pallas kernels, on_device(): pl.pallas_call(functools.partial(fused_kernel, tuple(scratch)), out_shape...  119 us

profile of v9, /device:TPU:14, one launch (start us, length us, event | category | flops | bytes accessed | tf_op | source)
XLA Modules:
  0.0 122.2 jit_solution(18311076449265577266)
XLA Ops:
  0.6 119.1 %shard_map.58 = (f32[512,256]{1,0:T(8,128)}, f32[32,512]{1,0:T(8,128)}, f32[768,256]{1,0:T(8,128)}) custom-call(f32[768,256]{1,0:T(8,128)} %mine_ref.1, f32[8,2,256,256]{3,2,1,0:T(8,128)} %bitcast.3, f32[8,2,256,512]{3,2,1,0:T(8,128)} %bitcast.2), custom_call_target="tpu_custom_call" | custom-call | flops 10000000000 | bytes 20000000 | tf_op jit(solution)/shard_map/pallas_call | solution.py:771
  119.7 2.4 %shard_map.59 = (f32[512,256]{1,0:T(8,128)}, f32[32,512]{1,0:T(8,128)}, f32[768,256]{1,0:T(8,128)}) custom-call(f32[512,256]{1,0:T(8,128)} %get-tuple-element.6.refs_0_, f32[32,512]{1,0:T(8,128)} %get-tuple-element.7.refs_1_, f32[768,256]{1,0:T(8,128)} %get-tuple-element.8.refs_2_), custom_call_target="tpu_custom_call" | custom-call | tf_op jit(solution)/shard_map/pallas_call | solution.py:757

commit v10 on v9

--- a/solution.py
+++ b/solution.py
@@ -160,7 +160,7 @@
         cut_in=dma((n_rows,)),
         share=dma((n_rows, 2)),
         shared=dma((n_rows, 2)),
-        local=dma((4,)),
+        local=dma((5,)),
         factor_send=dma,
         factor_recv=dma,
         part_send=dma((CHIPS,)),
@@ -256,8 +256,10 @@
     give_factor.start()
     for one in fetch:
         one.start()
-    got[chip] = mine_ref[...]
-    own_high, own_low = split(mine_ref[...])
+    keep = pltpu.make_async_copy(mine_ref, got.at[chip], v.local.at[4])
+    keep.start()
+    keep.wait()
+    own_high, own_low = split(got[chip])
     v.high[core] = own_high
     v.low[core] = own_low
     give_mine.wait_recv()
@@ -775,7 +777,7 @@
             jax.ShapeDtypeStruct((2 * width // n_cols, 2 * width), jnp.float32),
             jax.ShapeDtypeStruct((n, width), jnp.float32),
         ),
-        in_specs=[vmem, pl.BlockSpec(memory_space=pl.ANY), pl.BlockSpec(memory_space=pl.ANY)],
+        in_specs=[pl.BlockSpec(memory_space=pl.ANY)] * 3,
         out_specs=(vmem, vmem, vmem),
         scratch_shapes=list(scratch.values()),
         compiler_params=pltpu.CompilerParams(

time: 122 us -> 121 us (level)
  no operation moved by 1% of the time
where the time goes in v10:
time: 121 us
  Pallas kernels  121 us (100%)
    pallas_call x1, Pallas kernels, on_device(): pl.pallas_call(functools.partial(fused_kernel, tuple(scratch)), out_shape...  118 us
    pallas_call x1, Pallas kernels, finish(): pl.pallas_call(finish_kernel, out_shape=tuple((jax.ShapeDtypeStruct(a.sha...  2.42 us

profile of v10, /device:TPU:14, one launch (start us, length us, event | category | flops | bytes accessed | tf_op | source)
XLA Modules:
  0.0 121.3 jit_solution(2509411613180877251)
XLA Ops:
  0.6 118.3 %shard_map.58 = (f32[512,256]{1,0:T(8,128)}, f32[32,512]{1,0:T(8,128)}, f32[768,256]{1,0:T(8,128)}) custom-call(f32[768,256]{1,0:T(8,128)} %mine_ref.1, f32[8,2,256,256]{3,2,1,0:T(8,128)} %bitcast.3, f32[8,2,256,512]{3,2,1,0:T(8,128)} %bitcast.2), custom_call_target="tpu_custom_call" | custom-call | flops 10000000000 | bytes 20000000 | tf_op jit(solution)/shard_map/pallas_call | solution.py:773
  118.9 2.4 %shard_map.59 = (f32[512,256]{1,0:T(8,128)}, f32[32,512]{1,0:T(8,128)}, f32[768,256]{1,0:T(8,128)}) custom-call(f32[512,256]{1,0:T(8,128)} %get-tuple-element.6.refs_0_, f32[32,512]{1,0:T(8,128)} %get-tuple-element.7.refs_1_, f32[768,256]{1,0:T(8,128)} %get-tuple-element.8.refs_2_), custom_call_target="tpu_custom_call" | custom-call | tf_op jit(solution)/shard_map/pallas_call | solution.py:759
